TPU v7x, 32 devices: a whole 2x2x4 slice. The times are simulated.
32 devices in a mesh: stream: 2 (over x), batch: 8 (over z, y), mp: 2 (over core).
Axes of the slice: x: 2, y: 2, z: 4, core: 2. Of those that a mesh axis runs over, the one named last changes fastest.
Arguments:
- tokens: bfloat16 [2, 8, 512, 768], P('stream', 'batch', 'mp'), may hold values from -6 to 6
- segments: int32 [8, 512], P('batch'), may hold values from 0 to 7, never falling along the last dimension, each value on 1 to 128 neighbouring positions
- top_mask: int32 [8, 16, 8, 512], P(None, 'mp', 'batch'), may hold values 0 or 1
- positive: int32 [8, 16], P(None, 'mp'), may hold values from 0 to 63
- w_query: bfloat16 [2, 768, 768], P(None, None, 'mp'), may hold values from -0.02734375 to 0.02734375
- w_kv: bfloat16 [2, 2, 768, 768], P(None, None, None, 'mp'), may hold values from -0.21875 to 0.21875
- w_out: bfloat16 [2, 768, 768], P(None, None, 'mp'), may hold values from -1.75 to 1.75
- w_in: bfloat16 [2, 2, 768, 3072], P(None, None, None, 'mp'), may hold values from -0.21875 to 0.21875
- w_down: bfloat16 [2, 768, 3072], P(None, None, 'mp'), may hold values from -0.15625 to 0.15625
- gains: float32 [5, 768], replicated, may hold values from 0.5 to 1.5
- rel_bias: float32 [32, 12], P(None, 'mp'), may hold values from -4 to 4
- w_proj: bfloat16 [768, 128], replicated, may hold values from -0.21875 to 0.21875
Outputs:
- vectors: bfloat16 [2, 8, 512, 128], P('stream', 'batch', 'mp')
- query_loss: float32 [8, 16], P('batch', 'mp')
- grad_tokens: float32 [2, 8, 512, 768], P('stream', 'batch', 'mp')
- grad_query: float32 [2, 768, 768], P(None, 'batch', 'mp')
- grad_kv: float32 [2, 2, 768, 768], P(None, None, 'batch', 'mp')
- grad_out: float32 [2, 768, 768], P(None, 'batch', 'mp')
- grad_in: float32 [2, 2, 768, 3072], P(None, None, 'batch', 'mp')
- grad_down: float32 [2, 768, 3072], P(None, 'batch', 'mp')
- grad_gains: float32 [5, 768], P(None, 'batch')
- grad_bias: float32 [32, 12], P(None, 'mp')
- grad_proj: float32 [768, 128], P('batch')
Inputs may be any that keep to these rules, and one draw needn't show every extreme that they name: `segments`: in each row the ids rise from 0 to 7 in runs, each document 1 to 128 positions long, one exactly 128.
All inputs are finite; a program needn't handle non-finite values. No bound on the sum of `top_mask` on one device may be relied on, other than what follows from the above.
Results may differ from a plain program's by a relative error of at most 0.033.
Values may be sent and summed in bfloat16 or wider, within the bound.
A program may use at most 256 MiB of HBM per device.

v0:
```python
import math

import jax
import jax.numpy as jnp
from jax import lax
from jax.sharding import PartitionSpec as P

QLEN = 32
DOCS_ROW = 8


norm_eps = 1e-06
vector_eps = 1e-06
temper = 0.05
logit_scale = 32.0
bucket_edges = (12, 16, 23, 32, 46, 64, 91)
highest = lax.Precision.HIGHEST


def shifted(value, axis, steps):
    count = lax.axis_size(axis)
    leading, last = (max(0, -steps), min(count, count - steps))
    return lax.ppermute(value, axis, [(source, source + steps) for source in range(leading, last)])


def merged(part, axis, combine):
    gathered = jax.tree.map(lambda a: lax.all_gather(a, axis), part)

    def take(source):
        return jax.tree.map(lambda a: lax.dynamic_index_in_dim(a, source, 0, False), gathered)

    return lax.fori_loop(
        1, lax.axis_size(axis), lambda source, state: combine(state, take(source)), take(0)
    )


def offset_buckets(length):
    offsets = jnp.arange(2 * length - 1, dtype=jnp.int32) - (length - 1)
    magnitude = jnp.abs(offsets)
    far_bucket = jnp.full(offsets.shape, 8, jnp.int32)
    for threshold in bucket_edges:
        far_bucket = far_bucket + (magnitude >= threshold).astype(jnp.int32)
    bucket = jnp.where(magnitude < 8, magnitude, jnp.minimum(far_bucket, 15))
    return bucket + jnp.where(offsets > 0, 16, 0).astype(jnp.int32)


def toeplitz_grid(table, length):
    head_count = table.shape[0]
    tiled = jnp.tile(table, (1, length))
    padded = jnp.concatenate([tiled, jnp.zeros((head_count, length), table.dtype)], axis=1)
    grid = padded.reshape(head_count, length, 2 * length)[:, :, :length]
    return grid[:, ::-1, :]


def diagonal_sums(grid):
    head_count, length = (grid.shape[0], grid.shape[1])
    flipped = grid[:, ::-1, :]
    padded = jnp.concatenate([flipped, jnp.zeros(flipped.shape, flipped.dtype)], axis=2)
    flat = padded.reshape(head_count, 2 * length * length)[:, : length * (2 * length - 1)]
    return jnp.sum(flat.reshape(head_count, length, 2 * length - 1), axis=1)


def rms_scale(values, gain_row):
    return (
        values * lax.rsqrt(jnp.mean(values * values, axis=-1, keepdims=True) + norm_eps) * gain_row
    )


def gated_gelu(gate_up):
    return jax.nn.gelu(gate_up[0], approximate=True) * gate_up[1]


def normalize(values):
    return values * lax.rsqrt(jnp.sum(values * values, axis=-1, keepdims=True) + vector_eps)


def model_rows(values):
    return lax.all_gather(values, "mp", axis=1, tiled=True)


def model_share(partial_sum):
    return lax.psum_scatter(
        partial_sum.astype(jnp.bfloat16), "mp", scatter_dimension=1, tiled=True
    ).astype(jnp.float32)


def split_heads(values, head_count):
    return values.reshape(values.shape[0], values.shape[1], head_count, -1)


def attention_scores(queries, keys_part, bias_grid, same_doc, head_count):
    scores = (
        jnp.einsum(
            "rshe,rthe->rhst",
            split_heads(queries, head_count),
            split_heads(keys_part, head_count),
            preferred_element_type=jnp.float32,
        )
        + bias_grid[None]
    )
    return jnp.where(same_doc, scores, -1000000000.0)


def layer_forward(inputs, same_doc, bias_grid, head_count, weights_layer):
    query_weight, kv_weight, out_weight, in_weight, down_weight, gain_attn, gain_ffn = weights_layer
    normed = model_rows(rms_scale(inputs, gain_attn).astype(jnp.bfloat16))
    queries = jnp.einsum(
        "rsd,di->rsi", normed, query_weight, preferred_element_type=jnp.float32
    ).astype(jnp.bfloat16)
    key_value = jnp.einsum(
        "rsd,tdi->trsi", normed, kv_weight, preferred_element_type=jnp.float32
    ).astype(jnp.bfloat16)
    scores = attention_scores(queries, key_value[0], bias_grid, same_doc, head_count)
    log_total = jax.nn.logsumexp(scores, axis=-1, keepdims=True)
    soft_weights = jnp.exp(scores - log_total).astype(jnp.bfloat16)
    attended = jnp.einsum(
        "rhst,rthe->rshe",
        soft_weights,
        split_heads(key_value[1], head_count),
        preferred_element_type=jnp.float32,
    ).astype(jnp.bfloat16)
    attended = attended.reshape(queries.shape)
    middle = inputs + model_share(
        jnp.einsum("rsi,di->rsd", attended, out_weight, preferred_element_type=jnp.float32)
    )
    ffn_input = model_rows(rms_scale(middle, gain_ffn).astype(jnp.bfloat16))
    gate_up = jnp.einsum("rsd,tdf->trsf", ffn_input, in_weight, preferred_element_type=jnp.float32)
    hidden = gated_gelu(gate_up).astype(jnp.bfloat16)
    output = middle + model_share(
        jnp.einsum("rsf,df->rsd", hidden, down_weight, preferred_element_type=jnp.float32)
    )
    return (
        output,
        (
            inputs,
            normed,
            queries,
            key_value,
            log_total,
            attended,
            middle,
            ffn_input,
            gate_up,
            hidden,
        ),
    )


def layer_backward(grad_output, kept_state, same_doc, bias_grid, head_count, weights_layer):
    inputs, normed, queries, key_value, log_total, attended, middle, ffn_input, gate_up, hidden = (
        kept_state
    )
    query_weight, kv_weight, out_weight, in_weight, down_weight, gain_attn, gain_ffn = weights_layer
    grad_branch = model_rows(grad_output.astype(jnp.bfloat16))
    grad_hidden = jnp.einsum(
        "rsd,df->rsf", grad_branch, down_weight, preferred_element_type=jnp.float32
    )
    grad_down = jnp.einsum("rsd,rsf->df", grad_branch, hidden, preferred_element_type=jnp.float32)
    gate_back = jax.vjp(gated_gelu, gate_up)[1]
    grad_gate_up = gate_back(grad_hidden)[0].astype(jnp.bfloat16)
    grad_in = jnp.einsum(
        "rsd,trsf->tdf", ffn_input, grad_gate_up, preferred_element_type=jnp.float32
    )
    grad_ffn_input = model_share(
        jnp.einsum("trsf,tdf->rsd", grad_gate_up, in_weight, preferred_element_type=jnp.float32)
    )
    grad_mid_norm, grad_gain_ffn = jax.vjp(rms_scale, middle, gain_ffn)[1](grad_ffn_input)
    grad_middle = grad_output + grad_mid_norm
    grad_attn = model_rows(grad_middle.astype(jnp.bfloat16))
    grad_attended = jnp.einsum(
        "rsd,di->rsi", grad_attn, out_weight, preferred_element_type=jnp.float32
    ).astype(jnp.bfloat16)
    grad_out = jnp.einsum("rsd,rsi->di", grad_attn, attended, preferred_element_type=jnp.float32)
    scores = attention_scores(queries, key_value[0], bias_grid, same_doc, head_count)
    soft_weights = jnp.exp(scores - log_total)
    grad_soft = jnp.einsum(
        "rshe,rthe->rhst",
        split_heads(grad_attended, head_count),
        split_heads(key_value[1], head_count),
        preferred_element_type=jnp.float32,
    )
    grad_scores = (
        soft_weights * (grad_soft - jnp.sum(soft_weights * grad_soft, axis=-1, keepdims=True))
    ).astype(jnp.bfloat16)
    grad_bias_grid = jnp.sum(grad_scores, axis=0, dtype=jnp.float32)
    grad_queries = (
        jnp.einsum(
            "rhst,rthe->rshe",
            grad_scores,
            split_heads(key_value[0], head_count),
            preferred_element_type=jnp.float32,
        )
        .astype(jnp.bfloat16)
        .reshape(queries.shape)
    )
    grad_keys = (
        jnp.einsum(
            "rhst,rshe->rthe",
            grad_scores,
            split_heads(queries, head_count),
            preferred_element_type=jnp.float32,
        )
        .astype(jnp.bfloat16)
        .reshape(queries.shape)
    )
    grad_values = (
        jnp.einsum(
            "rhst,rshe->rthe",
            soft_weights.astype(jnp.bfloat16),
            split_heads(grad_attended, head_count),
            preferred_element_type=jnp.float32,
        )
        .astype(jnp.bfloat16)
        .reshape(queries.shape)
    )
    grad_key_value = jnp.stack([grad_keys, grad_values])
    grad_query = jnp.einsum("rsd,rsi->di", normed, grad_queries, preferred_element_type=jnp.float32)
    grad_kv = jnp.einsum(
        "rsd,trsi->tdi", normed, grad_key_value, preferred_element_type=jnp.float32
    )
    grad_normed = model_share(
        jnp.einsum("rsi,di->rsd", grad_queries, query_weight, preferred_element_type=jnp.float32)
        + jnp.einsum("trsi,tdi->rsd", grad_key_value, kv_weight, preferred_element_type=jnp.float32)
    )
    grad_in_norm, grad_gain_attn = jax.vjp(rms_scale, inputs, gain_attn)[1](grad_normed)
    return (
        grad_middle + grad_in_norm,
        (grad_query, grad_kv, grad_out, grad_in, grad_down),
        grad_gain_attn,
        grad_gain_ffn,
        grad_bias_grid,
    )


def combine_stats(earlier_stats, later_stats):
    top_both = jnp.maximum(earlier_stats[0], later_stats[0])
    summed = earlier_stats[1] * jnp.exp(earlier_stats[0] - top_both) + later_stats[1] * jnp.exp(
        later_stats[0] - top_both
    )
    return (top_both, summed, earlier_stats[2] + later_stats[2])


def on_device(
    tokens,
    segments,
    top_mask,
    positive,
    w_query,
    w_kv,
    w_out,
    w_in,
    w_down,
    gains,
    rel_bias,
    w_proj,
):
    stream_side = lax.axis_index("stream")
    batch_index = lax.axis_index("batch")
    hidden_state = tokens[0].astype(jnp.float32)
    row_count, share_len, model_width = hidden_state.shape
    length = share_len * lax.axis_size("mp")
    head_count = rel_bias.shape[1]
    layers = w_query.shape[0]
    query_segments = jnp.broadcast_to(
        jnp.arange(length, dtype=jnp.int32) // QLEN, (row_count, length)
    )
    row_segments = jnp.where(stream_side == 0, query_segments, segments)
    same_doc = (row_segments[:, :, None] == row_segments[:, None, :])[:, None]
    buckets = offset_buckets(length)
    table = jnp.transpose(jnp.take(rel_bias, buckets, axis=0), (1, 0))
    bias_grid = toeplitz_grid(table, length)
    layer_weights = []
    kept_layers = []
    for layer_index in range(layers):
        weights_layer = (
            w_query[layer_index],
            w_kv[layer_index],
            w_out[layer_index],
            w_in[layer_index],
            w_down[layer_index],
            gains[2 * layer_index],
            gains[2 * layer_index + 1],
        )
        layer_weights.append(weights_layer)
        hidden_state, kept_state = layer_forward(
            hidden_state, same_doc, bias_grid, head_count, weights_layer
        )
        kept_layers.append(kept_state)
    final_in = rms_scale(hidden_state, gains[2 * layers]).astype(jnp.bfloat16)
    projected = jnp.einsum("rsd,dp->rsp", final_in, w_proj, preferred_element_type=jnp.float32)
    unit_vectors, normalize_back = jax.vjp(normalize, projected)
    vectors = unit_vectors.astype(jnp.bfloat16)
    sent_half = shifted(vectors, "stream", 1)
    gathered = lax.all_gather(sent_half, "batch", axis=0, tiled=True)
    doc_full = lax.all_gather(vectors, "mp", axis=1, tiled=True)
    query_rows = gathered.shape[0]
    per_half = share_len // QLEN
    block_rows = math.gcd(query_rows, 8)
    block_count = query_rows // block_rows
    block_slots = block_rows * per_half
    block_tokens = block_slots * QLEN
    doc_tokens = row_count * length
    query_blocks = gathered.reshape(block_count, block_tokens, -1)
    mask_cols = jnp.transpose(top_mask.reshape(query_rows * per_half, doc_tokens), (1, 0)).astype(
        jnp.float32
    )
    mask_blocks = jnp.transpose(mask_cols.reshape(doc_tokens, block_count, block_slots), (1, 0, 2))
    doc_flat = doc_full.reshape(doc_tokens, -1)
    local_docs = row_count * DOCS_ROW
    doc_ids = (segments + DOCS_ROW * jnp.arange(row_count, dtype=jnp.int32)[:, None]).reshape(-1)
    doc_onehot = (jnp.arange(local_docs, dtype=jnp.int32)[:, None] == doc_ids[None, :]).astype(
        jnp.float32
    )

    def pooled_sums(query_block, mask_block):
        similarity = jnp.einsum(
            "tp,kp->tk", doc_flat, query_block, preferred_element_type=jnp.float32
        )
        mask_wide = jnp.broadcast_to(
            mask_block[:, :, None], (doc_tokens, block_slots, QLEN)
        ).reshape(doc_tokens, block_tokens)
        raised = jnp.exp(similarity / temper) * mask_wide
        totals = jnp.einsum("nt,tk->nk", doc_onehot, raised, precision=highest)
        return (raised, totals)

    def block_logits(inputs):
        raised, totals = pooled_sums(inputs[0], inputs[1])
        pooled = jnp.mean(
            (temper * jnp.log1p(totals)).reshape(local_docs, block_slots, QLEN), axis=-1
        )
        return logit_scale * pooled

    logit_blocks = lax.map(block_logits, (query_blocks, mask_blocks))
    logits = jnp.transpose(logit_blocks, (0, 2, 1)).reshape(query_rows, per_half, local_docs)
    global_docs = batch_index * local_docs + jnp.arange(local_docs, dtype=jnp.int32)
    is_positive = (global_docs[None, None, :] == positive[:, :, None]).astype(jnp.float32)
    top_local = jnp.max(logits, axis=-1)
    doc_side = stream_side == 1
    top_part = jnp.where(doc_side, top_local, -1e30)
    exp_part = jnp.where(doc_side, jnp.sum(jnp.exp(logits - top_local[..., None]), axis=-1), 0.0)
    chosen_part = jnp.where(doc_side, jnp.sum(logits * is_positive, axis=-1), 0.0)
    top_all, exp_all, chosen = merged(
        (top_part, exp_part, chosen_part), ("stream", "batch"), combine_stats
    )
    log_total = top_all + jnp.log(exp_all)
    losses = log_total - chosen
    query_loss = lax.dynamic_slice_in_dim(losses, batch_index * row_count, row_count, 0)
    grad_logits = jnp.exp(logits - log_total[..., None]) - is_positive
    grad_blocks = jnp.transpose(
        grad_logits.reshape(block_count, block_slots, local_docs), (0, 2, 1)
    )

    def block_back(doc_grad, inputs):
        query_block, mask_block, grad_block = inputs
        raised, totals = pooled_sums(query_block, mask_block)
        grad_wide = jnp.broadcast_to(
            grad_block[:, :, None], (local_docs, block_slots, QLEN)
        ).reshape(local_docs, block_tokens)
        factor = grad_wide * (logit_scale / QLEN) / (1.0 + totals)
        spread = jnp.einsum("nt,nk->tk", doc_onehot, factor, precision=highest)
        grad_sims = (raised * spread).astype(jnp.bfloat16)
        grad_block_query = jnp.einsum(
            "tk,tp->kp", grad_sims, doc_flat, preferred_element_type=jnp.float32
        )
        doc_grad = doc_grad + jnp.einsum(
            "tk,kp->tp", grad_sims, query_block, preferred_element_type=jnp.float32
        )
        return (doc_grad, grad_block_query)

    doc_grad, grad_query_blocks = lax.scan(
        block_back, jnp.zeros(doc_flat.shape, jnp.float32), (query_blocks, mask_blocks, grad_blocks)
    )
    summed_query = lax.psum_scatter(
        grad_query_blocks.reshape(query_rows, share_len, -1),
        "batch",
        scatter_dimension=0,
        tiled=True,
    ).astype(jnp.bfloat16)
    returned = shifted(summed_query, "stream", -1)
    doc_share = lax.psum_scatter(
        doc_grad.reshape(row_count, length, -1).astype(jnp.bfloat16),
        "mp",
        scatter_dimension=1,
        tiled=True,
    )
    grad_vectors = jnp.where(stream_side == 0, returned, doc_share)
    grad_projected = normalize_back(grad_vectors.astype(jnp.float32))[0].astype(jnp.bfloat16)
    grad_proj = jnp.einsum(
        "rsd,rsp->dp", final_in, grad_projected, preferred_element_type=jnp.float32
    )
    grad_final = jnp.einsum(
        "rsp,dp->rsd", grad_projected, w_proj, preferred_element_type=jnp.float32
    )
    grad_state, grad_gain_final = jax.vjp(rms_scale, hidden_state, gains[2 * layers])[1](grad_final)
    weight_grads = [None] * layers
    gain_grads = [None] * (2 * layers)
    bias_grid_grad = jnp.zeros(bias_grid.shape, jnp.float32)
    for layer_index in reversed(range(layers)):
        (
            grad_state,
            weight_grads[layer_index],
            gain_grads[2 * layer_index],
            gain_grads[2 * layer_index + 1],
            grid_part,
        ) = layer_backward(
            grad_state,
            kept_layers[layer_index],
            same_doc,
            bias_grid,
            head_count,
            layer_weights[layer_index],
        )
        bias_grid_grad = bias_grid_grad + grid_part
    grad_query = jnp.stack([member[0] for member in weight_grads])
    grad_kv = jnp.stack([member[1] for member in weight_grads])
    grad_out = jnp.stack([member[2] for member in weight_grads])
    grad_in = jnp.stack([member[3] for member in weight_grads])
    grad_down = jnp.stack([member[4] for member in weight_grads])
    grad_gains = jnp.stack(gain_grads + [grad_gain_final])
    grad_proj, grad_gains = (
        lax.psum(grad_proj.astype(jnp.bfloat16), "mp").astype(jnp.float32),
        lax.psum(grad_gains.astype(jnp.bfloat16), "mp").astype(jnp.float32),
    )
    offset_onehot = (
        buckets[:, None] == jnp.arange(rel_bias.shape[0], dtype=jnp.int32)[None, :]
    ).astype(jnp.float32)
    grad_bias_local = jnp.einsum(
        "hk,kb->bh", diagonal_sums(bias_grid_grad), offset_onehot, precision=highest
    )
    grad_bias = lax.psum(grad_bias_local, ("stream", "batch"))
    part_query, part_kv, part_out, part_in, part_down, part_proj, part_gains = (
        lax.psum_scatter(grad_query, "batch", scatter_dimension=1, tiled=True),
        lax.psum_scatter(grad_kv, "batch", scatter_dimension=2, tiled=True),
        lax.psum_scatter(grad_out, "batch", scatter_dimension=1, tiled=True),
        lax.psum_scatter(grad_in, "batch", scatter_dimension=2, tiled=True),
        lax.psum_scatter(grad_down, "batch", scatter_dimension=1, tiled=True),
        lax.psum_scatter(grad_proj, "batch", scatter_dimension=0, tiled=True),
        lax.psum_scatter(grad_gains, "batch", scatter_dimension=1, tiled=True),
    )
    red_query, red_kv, red_out, red_in, red_down, red_proj, red_gains = (
        lax.psum(part_query.astype(jnp.bfloat16), "stream").astype(jnp.float32),
        lax.psum(part_kv.astype(jnp.bfloat16), "stream").astype(jnp.float32),
        lax.psum(part_out.astype(jnp.bfloat16), "stream").astype(jnp.float32),
        lax.psum(part_in.astype(jnp.bfloat16), "stream").astype(jnp.float32),
        lax.psum(part_down.astype(jnp.bfloat16), "stream").astype(jnp.float32),
        lax.psum(part_proj.astype(jnp.bfloat16), "stream").astype(jnp.float32),
        lax.psum(part_gains.astype(jnp.bfloat16), "stream").astype(jnp.float32),
    )
    return (
        vectors[None],
        query_loss,
        grad_state[None],
        red_query,
        red_kv,
        red_out,
        red_in,
        red_down,
        red_gains,
        grad_bias,
        red_proj,
    )


def solution(mesh):
    placed = (
        P("stream", "batch", "mp", None),
        P("batch", None),
        P(None, "mp", "batch", None),
        P(None, "mp"),
        P(None, None, "mp"),
        P(None, None, None, "mp"),
        P(None, None, "mp"),
        P(None, None, None, "mp"),
        P(None, None, "mp"),
        P(),
        P(None, "mp"),
        P(),
    )
    return jax.shard_map(
        on_device,
        mesh=mesh,
        in_specs=placed,
        out_specs=(
            P("stream", "batch", "mp", None),
            P("batch", "mp"),
            P("stream", "batch", "mp", None),
            P(None, "batch", "mp"),
            P(None, None, "batch", "mp"),
            P(None, "batch", "mp"),
            P(None, None, "batch", "mp"),
            P(None, "batch", "mp"),
            P(None, "batch"),
            P(None, "mp"),
            P("batch", None),
        ),
        check_vma=False,
    )
```

profile of v0, /device:TPU:0, one launch (start us, length us, event | category | flops | bytes accessed | tf_op | source)
XLA Modules:
  0.0 1891.7 jit_solution(8573749621786281422)
XLA Ops:
  19.9 6.2 tile.4
  26.1 13.6 reshape.1240
  39.8 14.0 tile.10
  53.8 11.5 concatenate.6
  65.3 17.6 copy.157
  83.0 6.8 slice.118
  89.8 6.7 copy.150
  96.4 51.2 %rev.6 = f32[6,512,512]{1,2,0:T(8,128)} reverse(f32[6,512,512]{1,2,0:T(8,128)} %copy.150), dimensions={1} | reverse | bytes 12582912 | tf_op jit(solution)/shard_map/rev | solution.py:52
  147.6 4.0 fusion.257
  157.7 11.0 reduce-scatter.18.cloned.1.call-done
  173.6 4.8 fusion.10
  184.7 9.5 reduce-scatter.20.cloned.1.call-done
  201.3 4.4 fusion.258
  211.0 9.5 reduce-scatter.22.cloned.1.call-done
  225.4 4.5 fusion.12
  238.8 5.4 copy.100
  255.2 31.6 %all_gather.47 = bf16[8,256,128]{2,1,0:T(8,128)(2,1)S(1)} all-gather(bf16[1,256,128]{2,1,0:T(8,128)(2,1)S(1)} %copy.99), channel_id=1, replica_groups=mesh['stream'=2,'batch'=8,'mp'=2] {'batch'}, dimensions={0}, use_global_device_ids=true | all-gather | bytes 589824 | tf_op jit(solution)/shard_map/all_gather | solution.py:294
  293.9 41.8 %all_gather.50 = f32[16,8,8]{2,1,0:T(8,128)S(1)} all-gather(f32[1,8,8]{2,1,0:T(8,128)S(1)} %select_n.210), channel_id=1, replica_groups=mesh['stream'=2,'batch'=8,'mp'=2] {'stream','batch'}, dimensions={0}, use_global_device_ids=true | all-gather | bytes 4352 | tf_op jit(solution)/shard_map/all_gather | solution.py:27
  335.9 35.8 %all_gather.49 = f32[16,8,8]{2,1,0:T(8,128)S(1)} all-gather(f32[1,8,8]{2,1,0:T(8,128)S(1)} %select_n.208), channel_id=1, replica_groups=mesh['stream'=2,'batch'=8,'mp'=2] {'stream','batch'}, dimensions={0}, use_global_device_ids=true | all-gather | bytes 4352 | tf_op jit(solution)/shard_map/all_gather | solution.py:27
  371.7 37.8 %all_gather.48 = f32[16,8,8]{2,1,0:T(8,128)S(1)} all-gather(f32[1,8,8]{2,1,0:T(8,128)S(1)} %select_n.206), channel_id=1, replica_groups=mesh['stream'=2,'batch'=8,'mp'=2] {'stream','batch'}, dimensions={0}, use_global_device_ids=true | all-gather | bytes 4352 | tf_op jit(solution)/shard_map/all_gather | solution.py:27
  411.2 5.4 multiply_convert_fusion.2
  427.3 56.2 %reduce-scatter.26.cloned.1.call-done = f32[1,256,128]{1,2,0:T(8,128)} async-done(((f32[8,256,128]{1,2,0:T(8,128)}), f32[1,256,128]{1,2,0:T(8,128)}) %reduce-scatter.26.cloned.1.call-update) | async-done | bytes 131088 | tf_op jit(solution)/shard_map/reduce_scatter | solution.py:373
  485.7 7.1 reduce-scatter.28.cloned.1.call-done
  497.4 6.0 fusion.60
  509.9 11.2 reduce-scatter.30.cloned.1.call-done
  527.4 4.4 multiply_reduce_fusion.1
  544.3 9.5 reduce-scatter.32.cloned.1.call-done
  559.2 6.1 fusion.56
  572.0 9.1 reduce-scatter.34.cloned.1.call-done
  588.0 4.3 multiply_reduce_fusion
  593.6 3.9 convert_add_fusion
  622.7 4.5 pad_maximum_fusion.1
  634.9 9.3 convolution_bitcast_fusion
  646.5 5.1 convolution_bitcast_fusion.1
  651.7 6.8 pad_maximum_fusion
  658.6 28.6 %copy.122 = f32[2,2,768,1536]{3,1,0,2:T(2,128)} copy(f32[2,2,768,1536]{2,3,1,0:T(8,128)} %pad_maximum_fusion) | data formatting | bytes 37748736 | tf_op jit(solution)/shard_map/stack | solution.py:417
  691.9 8.2 copy.119
  700.1 986.4 %all-reduce.18 = (bf16[2,2,768,384]{3,1,0,2:T(2,128)(2,1)S(1)}, bf16[2,2,768,1536]{3,1,0,2:T(2,128)(2,1)}) all-reduce(f32[2,2,768,384]{3,1,0,2:T(2,128)} %copy.119, f32[2,2,768,1536]{3,1,0,2:T(2,128)} %copy.122), channel_id=14, replica_groups=mesh['stream'=2,'batch'=8,'mp'=2] {'batch'}, use_global_device_ids=true, to_apply=%region_36.37.clone | all-reduce | flops 5898240 | bytes 35389440
  1697.9 51.0 %rev.7 = f32[6,512,512]{1,2,0:T(8,128)} reverse(f32[6,512,512]{1,2,0:T(8,128)} %get-tuple-element.309), dimensions={1} | reverse | bytes 12582912 | tf_op jit(solution)/shard_map/rev | solution.py:57
  1748.9 6.7 copy.152
  1755.5 9.2 pad_bitcast_fusion
  1764.8 17.9 copy.154
  1782.7 11.6 slice.125
  1794.3 12.2 reshape.1242
  1806.5 14.1 reshape.1210
  1820.7 5.6 reduce_sum.268
  1826.7 40.0 %psum.77 = f32[32,6]{0,1:T(8,128)} all-reduce(f32[32,6]{0,1:T(8,128)S(1)} %fusion.183), channel_id=1, replica_groups=mesh['stream'=2,'batch'=8,'mp'=2] {'stream','batch'}, use_global_device_ids=true, to_apply=%region_53.54 | all-reduce | flops 192 | bytes 1536 | tf_op jit(solution)/shard_map/psum | solution.py:430
  1868.7 8.1 all-reduce.9
  (512 shorter events, 198.3 us)
Async XLA Ops:
  7.2 241.5 %copy-start = (bf16[768,128]{1,0:T(8,128)(2,1)S(1)}, bf16[768,128]{1,0:T(8,128)(2,1)}, u32[]{:S(2)}) copy-start(bf16[768,128]{1,0:T(8,128)(2,1)} %param.25) | copy-start | bytes 589828
  7.2 161.5 %reduce-scatter.18.cloned.1.call-start = ((), (), s32[]{:S(2)}) async-start(), calls=%async_computation.15 | async-start | bytes 1179648 | tf_op jit(solution)/shard_map/reduce_scatter | solution.py:82
  8.3 161.8 %copy-start.83 = (f32[768]{0:T(1024)}, f32[768]{0:T(1024)S(1)}, u32[]{:S(2)}) copy-start(f32[768]{0:T(1024)S(1)} %get-tuple-element.279) | copy-start | bytes 9220
  8.3 187.4 %copy-start.76 = (f32[768]{0:T(1024)}, f32[768]{0:T(1024)S(1)}, u32[]{:S(2)}) copy-start(f32[768]{0:T(1024)S(1)} %get-tuple-element.278) | copy-start | bytes 9220
  8.3 213.7 %copy-start.85 = (f32[768]{0:T(1024)}, f32[768]{0:T(1024)S(1)}, u32[]{:S(2)}) copy-start(f32[768]{0:T(1024)S(1)} %get-tuple-element.277) | copy-start | bytes 9220
  8.3 238.7 %copy-start.78 = (f32[768]{0:T(1024)}, f32[768]{0:T(1024)S(1)}, u32[]{:S(2)}) copy-start(f32[768]{0:T(1024)S(1)} %get-tuple-element.281) | copy-start | bytes 9220
  15.8 131.8 %copy-start.34 = (bf16[1,1,512,384]{2,3,0,1:T(8,128)(2,1)}, bf16[1,1,512,384]{2,3,0,1:T(8,128)(2,1)S(1)}, u32[]{:S(2)}) copy-start(bf16[1,1,512,384]{2,3,0,1:T(8,128)(2,1)S(1)} %get-tuple-element.326) | copy-start | bytes 1179652
  15.8 136.8 %copy-start.21 = (bf16[1,1,512,384]{2,3,0,1:T(8,128)(2,1)}, bf16[1,1,512,384]{2,3,0,1:T(8,128)(2,1)S(1)}, u32[]{:S(2)}) copy-start(bf16[1,1,512,384]{2,3,0,1:T(8,128)(2,1)S(1)} %get-tuple-element.327) | copy-start | bytes 1179652
  16.3 131.3 %copy-start.59 = (bf16[512,384]{0,1:T(8,128)(2,1)}, bf16[512,384]{0,1:T(8,128)(2,1)S(1)}, u32[]{:S(2)}) copy-start(bf16[512,384]{0,1:T(8,128)(2,1)S(1)} %convolution_convert_fusion.15) | copy-start | bytes 1179652
  154.3 14.4 copy-start.4
  157.7 36.5 %reduce-scatter.20.cloned.1.call-start = ((), (), s32[]{:S(2)}) async-start(), calls=%async_computation.16 | async-start | bytes 1179648 | tf_op jit(solution)/shard_map/reduce_scatter | solution.py:82
  168.7 13.6 slice-start.13
  184.7 35.8 %reduce-scatter.22.cloned.1.call-start = ((), (), s32[]{:S(2)}) async-start(), calls=%async_computation.17 | async-start | bytes 1179648 | tf_op jit(solution)/shard_map/reduce_scatter | solution.py:82
  210.9 34.8 %reduce-scatter.24.cloned.1.call-start = ((), (), s32[]{:S(2)}) async-start(), calls=%async_computation.18 | async-start | bytes 1179648 | tf_op jit(solution)/shard_map/reduce_scatter | solution.py:82
  236.2 247.3 %reduce-scatter.26.cloned.1.call-start = ((), (), s32[]{:S(2)}) async-start(), calls=%async_computation.19 | async-start | bytes 1179648 | tf_op jit(solution)/shard_map/reduce_scatter | solution.py:373
  248.7 41.2 %copy-start.30 = (bf16[256,768]{1,0:T(8,128)(2,1)}, bf16[256,768]{1,0:T(8,128)(2,1)S(1)}, u32[]{:S(2)}) copy-start(bf16[256,768]{1,0:T(8,128)(2,1)S(1)} %fusion.196) | copy-start | bytes 1179652
  249.6 5.5 collective-permute-start
  420.6 72.2 %copy-start.110 = (f32[256]{0:T(256)S(1)}, f32[256]{0:T(256)}, u32[]{:S(2)}) copy-start(f32[256]{0:T(256)} %copy-done.109) | copy-start | bytes 3076
  420.6 72.3 %copy-start.88 = (f32[256]{0:T(256)S(1)}, f32[256]{0:T(256)}, u32[]{:S(2)}) copy-start(f32[256]{0:T(256)} %copy-done.87) | copy-start | bytes 3076
  424.0 68.9 %copy-start.10 = (bf16[1,256,768]{2,1,0:T(8,128)(2,1)S(1)}, bf16[1,256,768]{2,1,0:T(8,128)(2,1)}, u32[]{:S(2)}) copy-start(bf16[1,256,768]{2,1,0:T(8,128)(2,1)} %reduce-scatter.24.cloned.1.call-done) | copy-start | bytes 1179652
  424.0 68.9 %copy-start.79 = (f32[768]{0:T(1024)S(1)}, f32[768]{0:T(1024)}, u32[]{:S(2)}) copy-start(f32[768]{0:T(1024)} %copy-done.78) | copy-start | bytes 9220
  424.0 68.9 %copy-start.93 = (f32[256]{0:T(256)S(1)}, f32[256]{0:T(256)}, u32[]{:S(2)}) copy-start(f32[256]{0:T(256)} %copy-done.92) | copy-start | bytes 3076
  424.0 69.9 %copy-start.114 = (f32[256]{0:T(256)S(1)}, f32[256]{0:T(256)}, u32[]{:S(2)}) copy-start(f32[256]{0:T(256)} %copy-done.113) | copy-start | bytes 3076
  424.0 68.7 %reduce-scatter.28.cloned.1.call-start = ((), (), s32[]{:S(2)}) async-start(), calls=%async_computation.20 | async-start | bytes 196608 | tf_op jit(solution)/shard_map/reduce_scatter | solution.py:380
  427.2 93.9 %reduce-scatter.30.cloned.1.call-start = ((), (), s32[]{:S(2)}) async-start(), calls=%async_computation.21 | async-start | bytes 1179648 | tf_op jit(solution)/shard_map/reduce_scatter | solution.py:82
  484.4 8.3 collective-permute-start.1
  506.3 14.8 copy-start.86
  506.3 14.8 copy-start.102
  506.3 16.2 copy-start.108
  506.3 16.2 copy-start.80
  506.3 16.2 copy-start.94
  509.9 44.0 %reduce-scatter.32.cloned.1.call-start = ((), (), s32[]{:S(2)}) async-start(), calls=%async_computation.22 | async-start | bytes 1179648 | tf_op jit(solution)/shard_map/reduce_scatter | solution.py:82
  544.3 36.8 %reduce-scatter.34.cloned.1.call-start = ((), (), s32[]{:S(2)}) async-start(), calls=%async_computation.23 | async-start | bytes 1179648 | tf_op jit(solution)/shard_map/reduce_scatter | solution.py:82
  553.9 14.1 slice-start.10
  568.0 14.6 copy-start.106
  568.0 14.6 copy-start.29
  571.5 57.6 %reduce-scatter.36.cloned.1.call-start = ((), (), s32[]{:S(2)}) async-start(), calls=%async_computation.24 | async-start | bytes 1179648 | tf_op jit(solution)/shard_map/reduce_scatter | solution.py:82
  606.6 37.6 %all-reduce.15.cloned.1.call-start = ((), (), s32[]{:S(2)}) async-start(), calls=%async_computation.28 | async-start | bytes 393216 | tf_op jit(solution)/shard_map/psum | solution.py:421
  607.7 1082.8 %reduce-scatter.40.cloned.1.call-start = ((), (), s32[]{:S(2)}) async-start(), calls=%async_computation.26 | async-start | bytes 2654208 | tf_op jit(solution)/shard_map/reduce_scatter | solution.py:434
  612.8 1079.3 %reduce-scatter.38.cloned.1.call-start = ((), (), s32[]{:S(2)}) async-start(), calls=%async_computation.25 | async-start | bytes 2654208 | tf_op jit(solution)/shard_map/reduce_scatter | solution.py:432
  617.8 1075.9 %reduce-scatter.42.cloned.1.call-start = ((), (), s32[]{:S(2)}) async-start(), calls=%async_computation.27 | async-start | bytes 10616832 | tf_op jit(solution)/shard_map/reduce_scatter | solution.py:436
  627.2 1240.6 %reduce-scatter.46.cloned.1.call-start = ((), (), s32[]{:S(2)}) async-start(), calls=%async_computation.30 | async-start | bytes 442368
  634.8 1233.9 %reduce-scatter.44.cloned.1.call-start = ((), (), s32[]{:S(2)}) async-start(), calls=%async_computation.29 | async-start | bytes 221184 | tf_op jit(solution)/shard_map/reduce_scatter | solution.py:437
  644.2 1233.9 %all-reduce.17.cloned.1.call-start = ((), (), s32[]{:S(2)}) async-start(), calls=%async_computation.31 | async-start | bytes 4718592 | tf_op jit(solution)/shard_map/psum | solution.py:442
  658.6 28.6 %copy-start.57 = (bf16[1,1,512,384]{3,2,0,1:T(8,128)(2,1)S(1)}, bf16[1,1,512,384]{3,2,0,1:T(8,128)(2,1)}, u32[]{:S(2)}) copy-start(bf16[1,1,512,384]{3,2,0,1:T(8,128)(2,1)} %copy-done.56) | copy-start | bytes 1179652
  1820.7 46.1 %copy-start.104 = (f32[256]{0:T(256)S(1)}, f32[256]{0:T(256)}, u32[]{:S(2)}) copy-start(f32[256]{0:T(256)} %copy-done.103) | copy-start | bytes 3076
  1820.7 46.1 %copy-start.46 = (f32[1,256,768]{2,1,0:T(8,128)S(1)}, f32[1,256,768]{2,1,0:T(8,128)}, u32[]{:S(2)}) copy-start(f32[1,256,768]{2,1,0:T(8,128)} %get-tuple-element.312) | copy-start | bytes 2359300
  1820.7 46.1 %copy-start.53 = (bf16[1,256,768]{2,1,0:T(8,128)(2,1)S(1)}, bf16[1,256,768]{2,1,0:T(8,128)(2,1)}, u32[]{:S(2)}) copy-start(bf16[1,256,768]{2,1,0:T(8,128)(2,1)} %reduce-scatter.36.cloned.1.call-done) | copy-start | bytes 1179652
  (110 other events, 550.2 us)
Sparse Core Ops, SparseCore 0:
  157.8 10.8 reduce-scatter.17
  184.8 9.3 reduce-scatter.19
  211.1 9.4 reduce-scatter.21
  236.3 9.3 reduce-scatter.23
  424.1 59.3 reduce-scatter.25
  486.2 6.4 reduce-scatter.27
  510.0 11.0 reduce-scatter.29
  544.4 9.4 reduce-scatter.31
  571.7 9.3 reduce-scatter.33
  606.7 9.4 reduce-scatter.35
  619.2 19.2 all-reduce.14
  642.2 70.1 reduce-scatter.39
  716.8 124.3 reduce-scatter.37
  845.1 286.6 reduce-scatter.41
  1135.2 93.7 reduce-scatter.45
  1232.5 99.6 reduce-scatter.43
  1696.0 68.0 all-reduce.16
where the time goes:
time: 1910 us; the launch traced here: 1890 us
  blocking collectives  1210 us (63%)
  local copies, waits for them, and re-layouts  344 us (18%)
  matrix products  125 us (7%)
  waiting for transfers between devices  124 us (6%)
  other arithmetic  69 us (4%)
    unnamed x1, blocking collectives  986 us
    all_gather x3, blocking collectives, merged(): gathered = jax.tree.map(lambda a: lax.all_gather(a, axis), part)  115 us
    unnamed x293, local copies, waits for them, and re-layouts  115 us
    reduce_scatter x8, waiting for transfers between devices, model_share(): lax.psum_scatter(partial_sum.astype(jnp.bfloat16), 'mp', scatter_dimensio...  60.2 us
    reduce_scatter x1, waiting for transfers between devices, on_device(): lax.psum_scatter(grad_query_blocks.reshape(query_rows, share_len, -1), 'b...  56.2 us
    rev x1, local copies, waits for them, and re-layouts, toeplitz_grid(): return grid[:, ::-1, :]  51.2 us
    rev x1, local copies, waits for them, and re-layouts, diagonal_sums(): flipped = grid[:, ::-1, :]  51 us
    psum x1, blocking collectives, on_device(): grad_bias = lax.psum(grad_bias_local, ('stream', 'batch'))  40 us
  transfers between devices with their start and end apart: 19, of which 9 were waited for; matrix products, arithmetic and copies ran while one was open for 13% of the time, Pallas kernels for 0%

commit v1 on v0

v1 whole, which is shorter than its diff:
```python
import functools
import math

import jax
import jax.numpy as jnp
from jax import lax
from jax.experimental import pallas as pl
from jax.experimental.pallas import tpu as pltpu
from jax.sharding import PartitionSpec as P

QLEN = 32
DOCS_ROW = 8
TILE = 128
SPAN = 512


norm_eps = 1e-06
vector_eps = 1e-06
temper = 0.05
logit_scale = 32.0
bucket_edges = (12, 16, 23, 32, 46, 64, 91)
highest = lax.Precision.HIGHEST
bf16 = jnp.bfloat16
f32 = jnp.float32


def dot(a, b):
    return lax.dot_general(a, b, (((1,), (0,)), ((), ())), preferred_element_type=f32)


def dot_nt(a, b):
    return lax.dot_general(a, b, (((1,), (1,)), ((), ())), preferred_element_type=f32)


def dot_tn(a, b):
    return lax.dot_general(a, b, (((0,), (0,)), ((), ())), preferred_element_type=f32)


def offset_buckets():
    index = jnp.arange(SPAN, dtype=jnp.int32)
    offsets = jnp.where(index < SPAN // 2, index, index - SPAN)
    magnitude = jnp.abs(offsets)
    far_bucket = jnp.full(offsets.shape, 8, jnp.int32)
    for threshold in bucket_edges:
        far_bucket = far_bucket + (magnitude >= threshold).astype(jnp.int32)
    bucket = jnp.where(magnitude < 8, magnitude, jnp.minimum(far_bucket, 15))
    return bucket + jnp.where(offsets > 0, 16, 0).astype(jnp.int32)


def window(tile, tiles):
    first, last = max(0, tile - 1), min(tiles, tile + 2)
    shift = first - (tile - 1)
    return pl.ds(first * TILE, (last - first) * TILE), slice(shift * TILE, (shift + last - first) * TILE)


def fill_masks(row_ids, col_ids, mask, tiles):
    for tile in range(tiles):
        rows = pl.ds(tile * TILE, TILE)
        own = col_ids[rows, :]
        for near in range(max(0, tile - 1), min(tiles, tile + 2)):
            other = jnp.broadcast_to(row_ids[0:1, near * TILE : (near + 1) * TILE], (TILE, TILE))
            place = (near - tile + 1) * TILE
            mask[rows, place : place + TILE] = jnp.where(own == other, 0.0, -1e30)


def bias_tile(table, head):
    line = jnp.broadcast_to(table[pl.ds(head, 1), :], (TILE, SPAN))
    return pltpu.roll(line, TILE, axis=1, stride=1, stride_axis=0)[:, : 3 * TILE]


def attend_kernel(table, row_ids, col_ids, q, k, v, o, lse, mask, bias):
    tiles = q.shape[0] // TILE
    fill_masks(row_ids, col_ids, mask, tiles)
    lane = lax.broadcasted_iota(jnp.int32, (TILE, TILE), 1)
    lse[...] = jnp.zeros(lse.shape, f32)

    def pair(p, carry):
        cols = pl.ds(pl.multiple_of(p * TILE, TILE), TILE)
        for half in range(2):
            bias[half] = bias_tile(table, 2 * p + half)
        for tile in range(tiles):
            rows = pl.ds(tile * TILE, TILE)
            keys, frame = window(tile, tiles)
            queries = q[rows, cols]
            near_keys, near_values = k[keys, cols], v[keys, cols]
            outs = []
            kept = lse[rows, :]
            for half in range(2):
                mine = (lane >= 64) if half else (lane < 64)
                s = dot_nt(jnp.where(mine, queries, jnp.zeros_like(queries)), near_keys)
                s = s + bias[half][:, frame] + mask[rows, frame]
                top = jnp.max(s, axis=-1, keepdims=True)
                e = jnp.exp(s - top)
                total = jnp.sum(e, axis=-1, keepdims=True)
                weights = (e * (1.0 / total)).astype(bf16)
                outs.append(dot(weights, near_values))
                kept = jnp.where(lane == 2 * p + half, top + jnp.log(total), kept)
            lse[rows, :] = kept
            o[rows, cols] = jnp.where(lane < 64, outs[0], outs[1]).astype(bf16)
        return carry

    lax.fori_loop(0, q.shape[1] // TILE, pair, 0)


def attend(table, row_ids, col_ids, q, k, v):
    length, width = q.shape
    return pl.pallas_call(
        attend_kernel,
        out_shape=(
            jax.ShapeDtypeStruct((length, width), bf16),
            jax.ShapeDtypeStruct((length, TILE), f32),
        ),
        scratch_shapes=[pltpu.VMEM((length, 3 * TILE), f32), pltpu.VMEM((2, TILE, 3 * TILE), f32)],
        compiler_params=pltpu.CompilerParams(vmem_limit_bytes=32 * 1024 * 1024),
        cost_estimate=pl.CostEstimate(flops=10**9, bytes_accessed=3 * 10**6, transcendentals=10**6),
        name="attend",
    )(table, row_ids, col_ids, q, k, v)


def attend_back_kernel(
    table, row_ids, col_ids, lse, q, k, v, do, dq, dk, dv, sums, mask, bias, grid, dk_sum, dv_sum
):
    tiles = q.shape[0] // TILE
    fill_masks(row_ids, col_ids, mask, tiles)
    lane = lax.broadcasted_iota(jnp.int32, (TILE, TILE), 1)
    row_index = lax.broadcasted_iota(jnp.int32, (TILE, SPAN), 0)
    sums[...] = jnp.zeros(sums.shape, f32)

    def pair(p, carry):
        cols = pl.ds(pl.multiple_of(p * TILE, TILE), TILE)
        for half in range(2):
            bias[half] = bias_tile(table, 2 * p + half)
        grid[...] = jnp.zeros(grid.shape, f32)
        dk_sum[...] = jnp.zeros(dk_sum.shape, f32)
        dv_sum[...] = jnp.zeros(dv_sum.shape, f32)
        for tile in range(tiles):
            rows = pl.ds(tile * TILE, TILE)
            keys, frame = window(tile, tiles)
            queries, grads = q[rows, cols], do[rows, cols]
            near_keys, near_values = k[keys, cols], v[keys, cols]
            kept = lse[rows, :]
            outs = []
            for half in range(2):
                mine = (lane >= 64) if half else (lane < 64)
                own_queries = jnp.where(mine, queries, jnp.zeros_like(queries))
                own_grads = jnp.where(mine, grads, jnp.zeros_like(grads))
                log_total = jnp.sum(
                    jnp.where(lane == 2 * p + half, kept, 0.0), axis=-1, keepdims=True
                )
                s = dot_nt(own_queries, near_keys)
                s = s + bias[half][:, frame] + mask[rows, frame]
                weights = jnp.exp(s - log_total)
                grad_weights = dot_nt(own_grads, near_values)
                mean = jnp.sum(weights * grad_weights, axis=-1, keepdims=True)
                ds = (weights * (grad_weights - mean)).astype(bf16)
                outs.append(dot(ds, near_keys))
                dk_sum[keys, :] += dot_tn(ds, own_queries)
                dv_sum[keys, :] += dot_tn(weights.astype(bf16), own_grads)
                grid[half, :, frame] += ds.astype(f32)
            dq[rows, cols] = jnp.where(lane < 64, outs[0], outs[1]).astype(bf16)
        dk[:, cols] = dk_sum[...].astype(bf16)
        dv[:, cols] = dv_sum[...].astype(bf16)
        for half in range(2):
            turned = pltpu.roll(grid[half], SPAN - TILE, axis=1)
            for bit in range(7):
                moved = pltpu.roll(turned, SPAN - (1 << bit), axis=1)
                turned = jnp.where((row_index >> bit) & 1 == 1, moved, turned)
            sums[pl.ds(2 * p + half, 1), :] = jnp.sum(turned, axis=0, keepdims=True)
        return carry

    lax.fori_loop(0, q.shape[1] // TILE, pair, 0)


def attend_back(table, row_ids, col_ids, lse, q, k, v, do):
    length, width = q.shape
    grad = jax.ShapeDtypeStruct((length, width), bf16)
    return pl.pallas_call(
        attend_back_kernel,
        out_shape=(grad, grad, grad, jax.ShapeDtypeStruct(table.shape, f32)),
        scratch_shapes=[
            pltpu.VMEM((length, 3 * TILE), f32),
            pltpu.VMEM((2, TILE, 3 * TILE), f32),
            pltpu.VMEM((2, TILE, SPAN), f32),
            pltpu.VMEM((length, TILE), f32),
            pltpu.VMEM((length, TILE), f32),
        ],
        compiler_params=pltpu.CompilerParams(vmem_limit_bytes=32 * 1024 * 1024),
        cost_estimate=pl.CostEstimate(flops=25 * 10**8, bytes_accessed=4 * 10**6, transcendentals=10**6),
        name="attend_back",
    )(table, row_ids, col_ids, lse, q, k, v, do)


def rms_scale(values, gain_row):
    return (
        values * lax.rsqrt(jnp.mean(values * values, axis=-1, keepdims=True) + norm_eps) * gain_row
    )


def gated_gelu(gate, up):
    return jax.nn.gelu(gate, approximate=True) * up


def normalize(values):
    return values * lax.rsqrt(jnp.sum(values * values, axis=-1, keepdims=True) + vector_eps)


def swap(value, axis):
    return lax.ppermute(value, axis, [(0, 1), (1, 0)])


def sum_of_two(part, axis):
    mine = lax.optimization_barrier(part.astype(bf16))
    return mine.astype(f32) + swap(mine, axis).astype(f32)


def layer_forward(inputs, table, row_ids, col_ids, weights_layer):
    query_weight, kv_weight, out_weight, in_weight, down_weight, gain_attn, gain_ffn = weights_layer
    normed = rms_scale(inputs, gain_attn).astype(bf16)
    q = dot(normed, query_weight).astype(bf16)
    k = dot(normed, kv_weight[0]).astype(bf16)
    v = dot(normed, kv_weight[1]).astype(bf16)
    attended, lse = attend(table, row_ids, col_ids, q, k, v)
    middle = inputs + sum_of_two(dot_nt(attended, out_weight), "mp")
    ffn_input = rms_scale(middle, gain_ffn).astype(bf16)
    gate, up = dot(ffn_input, in_weight[0]), dot(ffn_input, in_weight[1])
    hidden = gated_gelu(gate, up).astype(bf16)
    output = middle + sum_of_two(dot_nt(hidden, down_weight), "mp")
    return output, (inputs, normed, q, k, v, lse, attended, middle, ffn_input, gate, up, hidden)


def ffn_backward(grad_output, kept, weights_layer):
    middle, ffn_input, gate, up, hidden = kept[7:]
    in_weight, down_weight, gain_ffn = weights_layer[3], weights_layer[4], weights_layer[6]
    grad_branch = grad_output.astype(bf16)
    grad_hidden = dot(grad_branch, down_weight)
    grad_down = dot_tn(grad_branch, hidden).astype(bf16)
    grad_gate, grad_up = jax.vjp(gated_gelu, gate, up)[1](grad_hidden)
    grad_gate, grad_up = grad_gate.astype(bf16), grad_up.astype(bf16)
    grad_in = (dot_tn(ffn_input, grad_gate).astype(bf16), dot_tn(ffn_input, grad_up).astype(bf16))
    grad_input = sum_of_two(dot_nt(grad_gate, in_weight[0]) + dot_nt(grad_up, in_weight[1]), "mp")
    grad_mid_norm, grad_gain = jax.vjp(rms_scale, middle, gain_ffn)[1](grad_input)
    return grad_output + grad_mid_norm, grad_down, grad_in, grad_gain


def attention_backward(grad_middle, table, row_ids, col_ids, kept, weights_layer):
    inputs, normed, q, k, v, lse, attended = kept[:7]
    query_weight, kv_weight, out_weight, gain_attn = (
        weights_layer[0],
        weights_layer[1],
        weights_layer[2],
        weights_layer[5],
    )
    grad_attn = grad_middle.astype(bf16)
    do = dot(grad_attn, out_weight).astype(bf16)
    dq, dk, dv, sums = attend_back(table, row_ids, col_ids, lse, q, k, v, do)
    grads = [dot_tn(grad_attn, attended)] + [dot_tn(normed, part) for part in (dq, dk, dv)]
    grads = jnp.concatenate([part.astype(bf16) for part in grads], axis=1)
    grad_normed = sum_of_two(
        dot_nt(dq, query_weight) + dot_nt(dk, kv_weight[0]) + dot_nt(dv, kv_weight[1]), "mp"
    )
    grad_in_norm, grad_gain = jax.vjp(rms_scale, inputs, gain_attn)[1](grad_normed)
    return grad_middle + grad_in_norm, grads, grad_gain, sums


def pick(value, index, axis):
    return lax.dynamic_index_in_dim(value, index, axis, False)


def paired(sent, kept, axis, pairs):
    return (kept.astype(f32) + lax.ppermute(sent, axis, pairs).astype(f32)).astype(bf16)


def scatter_inner(part):
    inner = lax.axis_index("batch") % 2
    pairs = [(i, i ^ 1) for i in range(lax.axis_size("batch"))]
    return paired(pick(part, 1 - inner, 1), pick(part, inner, 1), "batch", pairs)


def scatter_outer(part):
    count = lax.axis_size("batch") // 2
    outer = lax.axis_index("batch") // 2
    total = pick(part, outer, 0).astype(f32)
    for step in range(1, count):
        pairs = [(i, ((i // 2 + step) % count) * 2 + i % 2) for i in range(2 * count)]
        total = total + lax.ppermute(pick(part, (outer + step) % count, 0), "batch", pairs).astype(f32)
    return lax.optimization_barrier(total.astype(bf16))


def reduce_rows(grad, streams_first):
    batch = lax.axis_size("batch")
    rows, columns = grad.shape[0] // batch, grad.shape[1]
    if batch % 2 or batch > 8:
        part = lax.psum_scatter(grad, "batch", scatter_dimension=0, tiled=True)
        return sum_of_two(part, "stream")
    if not streams_first:
        part = scatter_outer(scatter_inner(grad.reshape(batch // 2, 2, rows, columns)))
        return part.astype(f32) + swap(part, "stream").astype(f32)
    side = lax.axis_index("stream")
    half = columns // 2
    kept = lax.dynamic_slice_in_dim(grad, side * half, half, 1)
    sent = lax.dynamic_slice_in_dim(grad, (1 - side) * half, half, 1)
    part = paired(sent, kept, "stream", [(0, 1), (1, 0)])
    part = scatter_outer(scatter_inner(part.reshape(batch // 2, 2, rows, half)))
    other = swap(part, "stream")
    first = jnp.where(side == 0, part, other)
    last = jnp.where(side == 0, other, part)
    return jnp.concatenate([first, last], axis=1).astype(f32)


def on_device(
    tokens,
    segments,
    top_mask,
    positive,
    w_query,
    w_kv,
    w_out,
    w_in,
    w_down,
    gains,
    rel_bias,
    w_proj,
):
    stream_side = lax.axis_index("stream")
    batch_index = lax.axis_index("batch")
    mp_index = lax.axis_index("mp")
    row = lax.all_gather(tokens[0], "mp", axis=1, tiled=True)
    row_count, length, model_width = row.shape
    share_len = tokens.shape[2]
    hidden_state = row[0].astype(f32)
    head_count = rel_bias.shape[1]
    layers = w_query.shape[0]
    query_segments = jnp.arange(length, dtype=jnp.int32) // QLEN
    row_segments = jnp.where(stream_side == 0, query_segments, segments[0])
    row_ids = jnp.broadcast_to(row_segments[None, :], (8, length))
    col_ids = jnp.broadcast_to(row_segments[:, None], (length, TILE))
    offset_onehot = (
        offset_buckets()[None, :] == jnp.arange(rel_bias.shape[0], dtype=jnp.int32)[:, None]
    ).astype(f32)
    table = jnp.einsum(
        "bh,bk->hk", jnp.pad(rel_bias, ((0, 0), (0, 8 - head_count))), offset_onehot, precision=highest
    )
    layer_weights = []
    kept_layers = []
    for layer_index in range(layers):
        weights_layer = (
            w_query[layer_index],
            w_kv[layer_index],
            w_out[layer_index],
            w_in[layer_index],
            w_down[layer_index],
            gains[2 * layer_index],
            gains[2 * layer_index + 1],
        )
        layer_weights.append(weights_layer)
        hidden_state, kept_state = layer_forward(
            hidden_state, table, row_ids, col_ids, weights_layer
        )
        kept_layers.append(kept_state)
    final_in = rms_scale(hidden_state, gains[2 * layers]).astype(bf16)
    projected = dot(final_in, w_proj)
    unit_vectors, normalize_back = jax.vjp(normalize, projected)
    vectors = unit_vectors.astype(bf16)
    own_vectors = lax.dynamic_slice_in_dim(vectors, mp_index * share_len, share_len, 0)
    sent_half = lax.ppermute(own_vectors, "stream", [(0, 1)])
    gathered = lax.all_gather(sent_half, "batch", axis=0)
    query_rows = gathered.shape[0]
    per_half = share_len // QLEN
    block_rows = math.gcd(query_rows, 8)
    block_count = query_rows // block_rows
    block_slots = block_rows * per_half
    block_tokens = block_slots * QLEN
    doc_tokens = length
    query_blocks = gathered.reshape(block_count, block_tokens, -1)
    mask_cols = jnp.transpose(top_mask.reshape(query_rows * per_half, doc_tokens), (1, 0)).astype(
        f32
    )
    mask_blocks = jnp.transpose(mask_cols.reshape(doc_tokens, block_count, block_slots), (1, 0, 2))
    doc_flat = vectors
    local_docs = DOCS_ROW
    doc_ids = segments.reshape(-1)
    doc_onehot = (jnp.arange(local_docs, dtype=jnp.int32)[:, None] == doc_ids[None, :]).astype(f32)

    def pooled_sums(query_block, mask_block):
        similarity = dot_nt(doc_flat, query_block)
        mask_wide = jnp.broadcast_to(
            mask_block[:, :, None], (doc_tokens, block_slots, QLEN)
        ).reshape(doc_tokens, block_tokens)
        raised = jnp.exp(similarity / temper) * mask_wide
        totals = jnp.einsum("nt,tk->nk", doc_onehot, raised, precision=highest)
        return (raised, totals)

    def block_logits(inputs):
        raised, totals = pooled_sums(inputs[0], inputs[1])
        pooled = jnp.mean(
            (temper * jnp.log1p(totals)).reshape(local_docs, block_slots, QLEN), axis=-1
        )
        return logit_scale * pooled

    logit_blocks = lax.map(block_logits, (query_blocks, mask_blocks))
    logits = jnp.transpose(logit_blocks, (0, 2, 1)).reshape(query_rows, per_half, local_docs)
    global_docs = batch_index * local_docs + jnp.arange(local_docs, dtype=jnp.int32)
    is_positive = (global_docs[None, None, :] == positive[:, :, None]).astype(f32)
    doc_side = stream_side == 1
    stats = jnp.stack([jnp.sum(jnp.exp(logits), axis=-1), jnp.sum(logits * is_positive, axis=-1)])
    stats = lax.psum(jnp.where(doc_side, stats, 0.0), ("stream", "batch"))
    log_total = jnp.log(stats[0])
    losses = log_total - stats[1]
    query_loss = lax.dynamic_slice_in_dim(losses, batch_index * row_count, row_count, 0)
    grad_logits = jnp.exp(logits - log_total[..., None]) - is_positive
    grad_blocks = jnp.transpose(
        grad_logits.reshape(block_count, block_slots, local_docs), (0, 2, 1)
    )

    def block_back(doc_grad, inputs):
        query_block, mask_block, grad_block = inputs
        raised, totals = pooled_sums(query_block, mask_block)
        grad_wide = jnp.broadcast_to(
            grad_block[:, :, None], (local_docs, block_slots, QLEN)
        ).reshape(local_docs, block_tokens)
        factor = grad_wide * (logit_scale / QLEN) / (1.0 + totals)
        spread = jnp.einsum("nt,nk->tk", doc_onehot, factor, precision=highest)
        grad_sims = (raised * spread).astype(bf16)
        grad_block_query = dot_tn(grad_sims, doc_flat)
        doc_grad = doc_grad + dot(grad_sims, query_block)
        return (doc_grad, grad_block_query)

    doc_grad, grad_query_blocks = lax.scan(
        block_back, jnp.zeros(doc_flat.shape, f32), (query_blocks, mask_blocks, grad_blocks)
    )
    summed_query = lax.psum_scatter(
        grad_query_blocks.reshape(query_rows, share_len, -1).astype(bf16),
        "batch",
        scatter_dimension=0,
        tiled=False,
    )
    returned = lax.ppermute(summed_query, "stream", [(1, 0)])
    returned = lax.all_gather(returned, "mp", axis=0, tiled=True)
    grad_vectors = jnp.where(
        stream_side == 0, returned.astype(f32), sum_of_two(doc_grad, "mp").astype(bf16).astype(f32)
    )
    grad_projected = normalize_back(grad_vectors)[0].astype(bf16)
    grad_proj = dot_tn(final_in, grad_projected).astype(bf16)
    grad_final = dot_nt(grad_projected, w_proj)
    grad_state, grad_gain_final = jax.vjp(rms_scale, hidden_state, gains[2 * layers])[1](grad_final)
    gain_grads = [None] * (2 * layers)
    reduced = [None] * layers
    reduced_proj = None
    sums = jnp.zeros(table.shape, f32)
    for layer_index in reversed(range(layers)):
        kept, weights_layer = kept_layers[layer_index], layer_weights[layer_index]
        grad_state, grad_down, grad_in, gain_grads[2 * layer_index + 1] = ffn_backward(
            grad_state, kept, weights_layer
        )
        down = reduce_rows(grad_down, False)
        gate, up = reduce_rows(grad_in[0], True), reduce_rows(grad_in[1], True)
        grad_state, grads, gain_grads[2 * layer_index], part = attention_backward(
            grad_state, table, row_ids, col_ids, kept, weights_layer
        )
        sums = sums + part
        if reduced_proj is None:
            rest = reduce_rows(jnp.concatenate([grads, grad_proj], axis=1), False)
            reduced_proj = rest[:, grads.shape[1] :]
            rest = rest[:, : grads.shape[1]]
        else:
            rest = reduce_rows(grads, False)
        reduced[layer_index] = (down, jnp.stack([gate, up]), jnp.split(rest, 4, axis=1))
    grad_bias_local = jnp.einsum("hk,bk->bh", sums, offset_onehot, precision=highest)[:, :head_count]
    grad_gains = jnp.stack(gain_grads + [grad_gain_final])
    grad_bias, grad_gains = lax.psum((grad_bias_local, grad_gains), ("stream", "batch"))
    rows = model_width // lax.axis_size("batch")
    grad_state = lax.dynamic_slice_in_dim(grad_state, mp_index * share_len, share_len, 0)
    return (
        own_vectors[None, None],
        query_loss,
        grad_state[None, None],
        jnp.stack([member[2][1] for member in reduced]),
        jnp.stack([jnp.stack(member[2][2:]) for member in reduced]),
        jnp.stack([member[2][0] for member in reduced]),
        jnp.stack([member[1] for member in reduced]),
        jnp.stack([member[0] for member in reduced]),
        lax.dynamic_slice_in_dim(grad_gains, batch_index * rows, rows, 1),
        grad_bias,
        reduced_proj,
    )


def solution(mesh):
    placed = (
        P("stream", "batch", "mp", None),
        P("batch", None),
        P(None, "mp", "batch", None),
        P(None, "mp"),
        P(None, None, "mp"),
        P(None, None, None, "mp"),
        P(None, None, "mp"),
        P(None, None, None, "mp"),
        P(None, None, "mp"),
        P(),
        P(None, "mp"),
        P(),
    )
    return jax.shard_map(
        on_device,
        mesh=mesh,
        in_specs=placed,
        out_specs=(
            P("stream", "batch", "mp", None),
            P("batch", "mp"),
            P("stream", "batch", "mp", None),
            P(None, "batch", "mp"),
            P(None, None, "batch", "mp"),
            P(None, "batch", "mp"),
            P(None, None, "batch", "mp"),
            P(None, "batch", "mp"),
            P(None, "batch"),
            P(None, "mp"),
            P("batch", None),
        ),
        check_vma=False,
    )
```

time: 1910 us -> 679 us (0.36)
  blocking collectives: 1210 us -> 167 us
  local copies, waits for them, and re-layouts: 344 us -> 56.4 us
  waiting for transfers between devices: 124 us -> 205 us
  starting transfers between devices: 6.17 us -> 67.6 us
  matrix products: 125 us -> 72.2 us
  Pallas kernels: 0 us -> 41.7 us
  other arithmetic: 69 us -> 49.1 us
    unnamed x1 -> x0, blocking collectives: 986 us -> none
    ppermute x2 -> x55, waiting for transfers between devices: 0.01 us -> 155 us  [the longest x24 64.8 us: scatter_outer(): lax.ppermute(pick(part, (outer + step) % count, 0), 'batch', pairs)]
    all_gather x13 -> x3, blocking collectives: 169 us -> 37.2 us  [the longest x1 32 us: on_device(): gathered = lax.all_gather(sent_half, 'batch', axis=0)]
    unnamed x293 -> x227, local copies, waits for them, and re-layouts: 115 us -> 13.1 us
    rev x2 -> x0, local copies, waits for them, and re-layouts: 102 us -> none  [the longest x1 51.2 us: toeplitz_grid(): return grid[:, ::-1, :]]
    psum x3 -> x2, blocking collectives: 51.4 us -> 130 us  [the longest x1 86.7 us: on_device(): lax.psum((grad_bias_local, grad_gains), ('stream', 'batch'))]
    reduce_scatter x14 -> x1, waiting for transfers between devices: 124 us -> 50.1 us  [on_device(): lax.psum_scatter(grad_query_blocks.reshape(query_rows, share_len, -1).ast...]
    ppermute x2 -> x55, starting transfers between devices: 4.89 us -> 67.6 us  [the longest x24 35.9 us: scatter_outer(): lax.ppermute(pick(part, (outer + step) % count, 0), 'batch', pairs)]
  transfers between devices with their start and end apart: 19 -> 56, of which waited for: 9 -> 25; matrix products, arithmetic and copies ran while one was open for 13% -> 15% of each run, Pallas kernels for 0% -> 4%
where the time goes in v1:
time: 679 us; the launch traced here: 675 us
  waiting for transfers between devices  205 us (30%)
  blocking collectives  167 us (25%)
  matrix products  72.2 us (11%)
  starting transfers between devices  67.6 us (10%)
  local copies, waits for them, and re-layouts  56.4 us (8%)
  other arithmetic  49.1 us (7%)
  Pallas kernels  41.7 us (6%)
  between operations  16.2 us (2%)
    psum x1, blocking collectives, on_device(): lax.psum((grad_bias_local, grad_gains), ('stream', 'batch'))  86.7 us
    ppermute x24, waiting for transfers between devices, scatter_outer(): lax.ppermute(pick(part, (outer + step) % count, 0), 'batch', pairs)  64.8 us
    ppermute x17, waiting for transfers between devices, swap(): return lax.ppermute(value, axis, [(0, 1), (1, 0)])  63.4 us
    reduce_scatter x1, waiting for transfers between devices, on_device(): lax.psum_scatter(grad_query_blocks.reshape(query_rows, share_len, -1).ast...  50.1 us
    psum x1, blocking collectives, on_device(): stats = lax.psum(jnp.where(doc_side, stats, 0.0), ('stream', 'batch'))  43 us
    ppermute x24, starting transfers between devices, scatter_outer(): lax.ppermute(pick(part, (outer + step) % count, 0), 'batch', pairs)  35.9 us
    all_gather x1, blocking collectives, on_device(): gathered = lax.all_gather(sent_half, 'batch', axis=0)  32 us
    dot_general x16, matrix products, dot(): lax.dot_general(a, b, (((1,), (0,)), ((), ())), preferred_element_type=f32)  31 us
  transfers between devices with their start and end apart: 56, of which 25 were waited for; matrix products, arithmetic and copies ran while one was open for 15% of the time, Pallas kernels for 4%

profile of v1, /device:TPU:0, one launch (start us, length us, event | category | flops | bytes accessed | tf_op | source)
XLA Modules:
  0.0 675.1 jit_solution(3068440216117872666)
XLA Ops:
  7.2 2.8 all-gather
  16.8 8.7 %attend.2 = (bf16[512,384]{1,0:T(8,128)(2,1)S(1)}, f32[512,128]{1,0:T(8,128)S(1)}) custom-call(f32[8,512]{1,0:T(8,128)S(1)} %fusion.168.table, s32[8,512]{1,0:T(8,128)S(1)} %broadcast_in_dim.67.row_ids, s32[512,128]{1,0:T(8,128)S(1)} %broadcast_in_dim.68.col_ids, bf16[512,384]{1,0:T(8,128)(2,1)S(1)} %convolution_convert_fusion.24.q, ...), custom_call_target="tpu_custom_call" | custom-call | flops 1000000000 | bytes 3000000 | tf_op jit(solution)/shard_map/attend/pallas_call | solution.py:107
  30.7 3.1 multiply_convert_fusion.4
  41.7 8.5 %attend.3 = (bf16[512,384]{1,0:T(8,128)(2,1)S(1)}, f32[512,128]{1,0:T(8,128)S(1)}) custom-call(f32[8,512]{1,0:T(8,128)S(1)} %fusion.168.table, s32[8,512]{1,0:T(8,128)S(1)} %broadcast_in_dim.67.row_ids, s32[512,128]{1,0:T(8,128)S(1)} %broadcast_in_dim.68.col_ids, bf16[512,384]{1,0:T(8,128)(2,1)S(1)} %convolution_convert_fusion.21.q, ...), custom_call_target="tpu_custom_call" | custom-call | flops 1000000000 | bytes 3000000 | tf_op jit(solution)/shard_map/attend/pallas_call | solution.py:107
  56.4 3.4 multiply_convert_fusion.3
  59.8 2.3 fusion.81
  63.5 2.5 broadcast_in_dim.106
  66.1 5.4 copy.36
  71.5 2.4 multiply_reduce_fusion.8
  74.6 4.5 collective-permute-start.4
  81.0 32.0 %all-gather.1 = bf16[2048,128]{0,1:T(8,128)(2,1)S(1)} all-gather(bf16[256,128]{0,1:T(8,128)(2,1)S(1)} %collective-permute-done.4), channel_id=3, replica_groups=mesh['stream'=2,'batch'=8,'mp'=2] {'batch'}, dimensions={0}, use_global_device_ids=true | all-gather | bytes 589824 | tf_op jit(solution)/shard_map/all_gather | solution.py:366
  113.8 2.1 log-plus-one_multiply_fusion
  119.0 43.0 %psum.21 = f32[2,8,8]{2,1,0:T(8,128)S(1)} all-reduce(f32[2,8,8]{2,1,0:T(8,128)S(1)} %maximum_select_fusion), channel_id=1, replica_groups=mesh['stream'=2,'batch'=8,'mp'=2] {'stream','batch'}, use_global_device_ids=true, to_apply=%region_9.10 | all-reduce | flops 128 | bytes 1024 | tf_op jit(solution)/shard_map/psum | solution.py:406
  166.0 4.2 multiply_convert_fusion
  174.6 2.4 convert_bitcast_fusion.1
  178.6 3.2 convolution_convert_fusion.26
  181.8 50.1 %reduce-scatter.2.cloned.1.call-done = bf16[1,256,128]{1,2,0:T(8,128)(2,1)} async-done(((bf16[8,256,128]{1,2,0:T(8,128)(2,1)}), bf16[1,256,128]{1,2,0:T(8,128)(2,1)}) %reduce-scatter.2.cloned.1.call-update) | async-done | bytes 65552 | tf_op jit(solution)/shard_map/reduce_scatter | solution.py:431
  234.5 3.9 collective-permute-done.5
  238.4 2.4 all_gather.15
  246.0 5.1 fusion.13
  269.2 12.4 %attend_back.2 = (bf16[512,384]{1,0:T(8,128)(2,1)S(1)}, bf16[512,384]{1,0:T(8,128)(2,1)S(1)}, bf16[512,384]{1,0:T(8,128)(2,1)S(1)}, f32[8,512]{1,0:T(8,128)S(1)}) custom-call(f32[8,512]{1,0:T(8,128)S(1)} %fusion.168.table, s32[8,512]{1,0:T(8,128)S(1)} %broadcast_in_dim.67.row_ids, s32[512,128]{1,0:T(8,128)S(1)} %broadcast_in_dim.68.col_ids, ...), custom_call_target="tpu_custom_call" | custom-call | flops 2500000000 | bytes 4000000 | tf_op jit(solution)/shard_map/attend_back/pallas_call | solution.py:177
  290.1 4.5 copy.40
  304.0 7.9 %collective-permute-done.33 = bf16[768,768]{1,0:T(8,128)(2,1)} collective-permute-done((bf16[768,768]{1,0:T(8,128)(2,1)}, bf16[768,768]{1,0:T(8,128)(2,1)}, u32[]{:S(2)}, u32[]{:S(2)}) %collective-permute-start.33) | collective-permute-done | bytes 1179680 | tf_op jit(solution)/shard_map/ppermute | solution.py:270
  316.8 11.3 %collective-permute-done.52 = bf16[96,1536]{1,0:T(8,128)(2,1)S(1)} collective-permute-done((bf16[96,1536]{1,0:T(8,128)(2,1)S(1)}, bf16[96,1536]{1,0:T(8,128)(2,1)S(1)}, u32[]{:S(2)}, u32[]{:S(2)}) %collective-permute-start.52) | collective-permute-done | bytes 294944 | tf_op jit(solution)/shard_map/ppermute | solution.py:285
  332.3 5.1 fusion.6
  358.6 6.9 %collective-permute-done.42 = bf16[96,768]{1,0:T(8,128)(2,1)S(1)} collective-permute-done((bf16[96,768]{1,0:T(8,128)(2,1)S(1)}, bf16[96,768]{1,0:T(8,128)(2,1)S(1)}, u32[]{:S(2)}, u32[]{:S(2)}) %collective-permute-start.42) | collective-permute-done | bytes 147488 | tf_op jit(solution)/shard_map/ppermute | solution.py:285
  365.5 5.9 collective-permute-start.35
  373.0 4.1 collective-permute-done.36
  379.2 48.5 %collective-permute-done.44 = bf16[96,768]{1,0:T(8,128)(2,1)S(1)} collective-permute-done((bf16[96,768]{1,0:T(8,128)(2,1)S(1)}, bf16[96,768]{1,0:T(8,128)(2,1)S(1)}, u32[]{:S(2)}, u32[]{:S(2)}) %collective-permute-start.44) | collective-permute-done | bytes 147488 | tf_op jit(solution)/shard_map/ppermute | solution.py:208
  429.2 3.7 collective-permute-done.38
  434.3 4.6 collective-permute-start.18
  441.8 12.2 %attend_back.3 = (bf16[512,384]{1,0:T(8,128)(2,1)S(1)}, bf16[512,384]{1,0:T(8,128)(2,1)S(1)}, bf16[512,384]{1,0:T(8,128)(2,1)S(1)}, f32[8,512]{1,0:T(8,128)S(1)}) custom-call(f32[8,512]{1,0:T(8,128)S(1)} %fusion.168.table, s32[8,512]{1,0:T(8,128)S(1)} %broadcast_in_dim.67.row_ids, s32[512,128]{1,0:T(8,128)S(1)} %broadcast_in_dim.68.col_ids, ...), custom_call_target="tpu_custom_call" | custom-call | flops 2500000000 | bytes 4000000 | tf_op jit(solution)/shard_map/attend_back/pallas_call | solution.py:177
  462.0 2.4 collective-permute-done.18
  466.6 4.3 copy.39
  470.9 2.5 dynamic-slice_bitcast_fusion.3
  478.8 11.5 %collective-permute-done.45 = bf16[4,96,1536]{2,1,0:T(8,128)(2,1)} collective-permute-done((bf16[4,96,1536]{2,1,0:T(8,128)(2,1)}, bf16[4,96,1536]{2,1,0:T(8,128)(2,1)}, u32[]{:S(2)}, u32[]{:S(2)}) %collective-permute-start.45) | collective-permute-done | bytes 1179680 | tf_op jit(solution)/shard_map/ppermute | solution.py:270
  492.1 3.8 collective-permute-start.48
  503.8 9.3 %collective-permute-done.47 = bf16[96,1536]{1,0:T(8,128)(2,1)S(1)} collective-permute-done((bf16[96,1536]{1,0:T(8,128)(2,1)S(1)}, bf16[96,1536]{1,0:T(8,128)(2,1)S(1)}, u32[]{:S(2)}, u32[]{:S(2)}) %collective-permute-start.47) | collective-permute-done | bytes 294944 | tf_op jit(solution)/shard_map/ppermute | solution.py:285
  516.0 3.0 fusion.61
  519.0 86.7 %all-reduce.1 = (f32[5,768]{1,0:T(8,128)S(1)}, f32[32,6]{0,1:T(8,128)}) all-reduce(f32[5,768]{1,0:T(8,128)S(1)} %stack.124, f32[32,6]{0,1:T(8,128)S(1)} %fusion.167), channel_id=1, replica_groups=mesh['stream'=2,'batch'=8,'mp'=2] {'stream','batch'}, use_global_device_ids=true, to_apply=%region_22.23 | all-reduce | flops 4032 | bytes 32256 | tf_op jit(solution)/shard_map/psum | solution.py:470
  606.4 2.5 fusion.94
  615.9 2.4 collective-permute-start.25
  620.2 7.4 %collective-permute-done.30 = bf16[96,768]{1,0:T(8,128)(2,1)S(1)} collective-permute-done((bf16[96,768]{1,0:T(8,128)(2,1)S(1)}, bf16[96,768]{1,0:T(8,128)(2,1)S(1)}, u32[]{:S(2)}, u32[]{:S(2)}) %collective-permute-start.30) | collective-permute-done | bytes 147488 | tf_op jit(solution)/shard_map/ppermute | solution.py:285
  629.1 2.1 collective-permute-start.32
  631.2 7.4 %collective-permute-done.24 = bf16[96,768]{1,0:T(8,128)(2,1)S(1)} collective-permute-done((bf16[96,768]{1,0:T(8,128)(2,1)S(1)}, bf16[96,768]{1,0:T(8,128)(2,1)S(1)}, u32[]{:S(2)}, u32[]{:S(2)}) %collective-permute-start.24) | collective-permute-done | bytes 147488 | tf_op jit(solution)/shard_map/ppermute | solution.py:285
  642.4 2.1 collective-permute-start.13
  648.2 10.4 %collective-permute-done.13 = bf16[96,1536]{1,0:T(8,128)(2,1)S(1)} collective-permute-done((bf16[96,1536]{1,0:T(8,128)(2,1)S(1)}, bf16[96,1536]{1,0:T(8,128)(2,1)S(1)}, u32[]{:S(2)}, u32[]{:S(2)}) %collective-permute-start.13) | collective-permute-done | bytes 294944 | tf_op jit(solution)/shard_map/ppermute | solution.py:285
  661.5 4.0 collective-permute-done.15
  (486 shorter events, 178.0 us)
Async XLA Ops:
  7.2 224.7 %reduce-scatter.2.cloned.1.call-start = ((), (), s32[]{:S(2)}) async-start(), calls=%async_computation.1 | async-start | bytes 589824 | tf_op jit(solution)/shard_map/reduce_scatter | solution.py:431
  62.1 9.4 %collective-permute-start.3 = (bf16[512,768]{1,0:T(8,128)(2,1)}, bf16[512,768]{1,0:T(8,128)(2,1)}, u32[]{:S(2)}, u32[]{:S(2)}) collective-permute-start(bf16[512,768]{1,0:T(8,128)(2,1)} %fusion.81), channel_id=1, source_target_pairs={{0,1},{1,0},{2,3},{3,2},{4,5},{5,4},{6,7},{7,6},{8,9},{9,8},{10,11... | collective-permute-start | bytes 2359304 | tf_op jit(solution)/shard_map/ppermute | solution.py:208
  181.8 59.0 %collective-permute-start.6 = (bf16[512,128]{0,1:T(8,128)(2,1)}, bf16[512,128]{0,1:T(8,128)(2,1)}, u32[]{:S(2)}, u32[]{:S(2)}) collective-permute-start(bf16[512,128]{0,1:T(8,128)(2,1)} %convolution_convert_fusion.26), channel_id=1, source_target_pairs={{0,1},{1,0},{2,3},{3,2},{4,5},{5,4},{6,7},{7,6},{8,9},{9,8},{10,11... | collective-permute-start | bytes 393224 | tf_op jit(solution)/shard_map/ppermute | solution.py:208
  256.8 8.4 %collective-permute-start.7 = (bf16[512,768]{1,0:T(8,128)(2,1)S(1)}, bf16[512,768]{1,0:T(8,128)(2,1)S(1)}, u32[]{:S(2)}, u32[]{:S(2)}) collective-permute-start(bf16[512,768]{1,0:T(8,128)(2,1)S(1)} %add_convert_fusion.7), channel_id=1, source_target_pairs={{0,1},{1,0},{2,3},{3,2},{4,5},{5,4},{6,7},{7,6},{8,9},{9,8},{10,11... | collective-permute-start | bytes 2359304 | tf_op jit(solution)/shard_map/ppermute | solution.py:208
  258.2 42.9 %collective-permute-start.39 = (bf16[768,768]{1,0:T(8,128)(2,1)}, bf16[768,768]{1,0:T(8,128)(2,1)}, u32[]{:S(2)}, u32[]{:S(2)}) collective-permute-start(bf16[768,768]{1,0:T(8,128)(2,1)} %constant_dynamic-slice_fusion.1), channel_id=1, source_target_pairs={{0,16},{16,0},{1,17},{17,1},{2,18},{18,2},{3,19},{19,3},{4,20},{20... | collective-permute-start | bytes 3538952 | tf_op jit(solution)/shard_map/ppermute | solution.py:270
  259.3 52.7 %collective-permute-start.33 = (bf16[768,768]{1,0:T(8,128)(2,1)}, bf16[768,768]{1,0:T(8,128)(2,1)}, u32[]{:S(2)}, u32[]{:S(2)}) collective-permute-start(bf16[768,768]{1,0:T(8,128)(2,1)} %constant_dynamic-slice_fusion.2), channel_id=1, source_target_pairs={{0,16},{16,0},{1,17},{17,1},{2,18},{18,2},{3,19},{19,3},{4,20},{20... | collective-permute-start | bytes 3538952 | tf_op jit(solution)/shard_map/ppermute | solution.py:270
  263.9 33.7 %collective-permute-start.50 = (bf16[4,96,1536]{2,1,0:T(8,128)(2,1)}, bf16[4,96,1536]{2,1,0:T(8,128)(2,1)}, u32[]{:S(2)}, u32[]{:S(2)}) collective-permute-start(bf16[4,96,1536]{2,1,0:T(8,128)(2,1)} %dynamic-slice_bitcast_fusion.1), channel_id=1, source_target_pairs={{0,2},{2,0},{4,6},{6,4},{8,10},{10,8},{12,14},{14,12},{1,3},{3,1},... | collective-permute-start | bytes 3538952 | tf_op jit(solution)/shard_map/ppermute | solution.py:270
  284.5 44.6 %collective-permute-start.8 = (bf16[512,768]{1,0:T(8,128)(2,1)S(1)}, bf16[512,768]{1,0:T(8,128)(2,1)S(1)}, u32[]{:S(2)}, u32[]{:S(2)}) collective-permute-start(bf16[512,768]{1,0:T(8,128)(2,1)S(1)} %add_convert_fusion.6), channel_id=1, source_target_pairs={{0,1},{1,0},{2,3},{3,2},{4,5},{5,4},{6,7},{7,6},{8,9},{9,8},{10,11... | collective-permute-start | bytes 2359304 | tf_op jit(solution)/shard_map/ppermute | solution.py:208
  296.2 137.5 %collective-permute-start.16 = (bf16[4,96,1664]{2,1,0:T(8,128)(2,1)S(1)}, bf16[4,96,1664]{2,1,0:T(8,128)(2,1)S(1)}, u32[]{:S(2)}, u32[]{:S(2)}) collective-permute-start(bf16[4,96,1664]{2,1,0:T(8,128)(2,1)S(1)} %dynamic-slice_bitcast_fusion), channel_id=1, source_target_pairs={{0,2},{2,0},{4,6},{6,4},{8,10},{10,8},{12,14},{14,12},{1,3},{3,1},... | collective-permute-start | bytes 3833864 | tf_op jit(solution)/shard_map/ppermute | solution.py:270
  299.4 15.9 %collective-permute-start.53 = (bf16[96,1536]{1,0:T(8,128)(2,1)S(1)}, bf16[96,1536]{1,0:T(8,128)(2,1)S(1)}, u32[]{:S(2)}, u32[]{:S(2)}) collective-permute-start(bf16[96,1536]{1,0:T(8,128)(2,1)S(1)} %get-tuple-element.116), channel_id=1, source_target_pairs={{0,12},{2,14},{4,0},{6,2},{8,4},{10,6},{12,8},{14,10},{1,13},{3,15... | collective-permute-start | bytes 884744 | tf_op jit(solution)/shard_map/ppermute | solution.py:285
  301.1 27.1 %collective-permute-start.52 = (bf16[96,1536]{1,0:T(8,128)(2,1)S(1)}, bf16[96,1536]{1,0:T(8,128)(2,1)S(1)}, u32[]{:S(2)}, u32[]{:S(2)}) collective-permute-start(bf16[96,1536]{1,0:T(8,128)(2,1)S(1)} %get-tuple-element.117), channel_id=1, source_target_pairs={{0,8},{2,10},{4,12},{6,14},{8,0},{10,2},{12,4},{14,6},{1,9},{3,11}... | collective-permute-start | bytes 884744 | tf_op jit(solution)/shard_map/ppermute | solution.py:285
  312.0 16.8 %collective-permute-start.51 = (bf16[96,1536]{1,0:T(8,128)(2,1)S(1)}, bf16[96,1536]{1,0:T(8,128)(2,1)S(1)}, u32[]{:S(2)}, u32[]{:S(2)}) collective-permute-start(bf16[96,1536]{1,0:T(8,128)(2,1)S(1)} %get-tuple-element.115), channel_id=1, source_target_pairs={{0,4},{2,6},{4,8},{6,10},{8,12},{10,14},{12,0},{14,2},{1,5},{3,7},... | collective-permute-start | bytes 884744 | tf_op jit(solution)/shard_map/ppermute | solution.py:285
  315.2 33.7 %collective-permute-start.40 = (bf16[4,96,768]{2,1,0:T(8,128)(2,1)S(1)}, bf16[4,96,768]{2,1,0:T(8,128)(2,1)S(1)}, u32[]{:S(2)}, u32[]{:S(2)}) collective-permute-start(bf16[4,96,768]{2,1,0:T(8,128)(2,1)S(1)} %dynamic-slice_bitcast_fusion.4), channel_id=1, source_target_pairs={{0,2},{2,0},{4,6},{6,4},{8,10},{10,8},{12,14},{14,12},{1,3},{3,1},... | collective-permute-start | bytes 1769480 | tf_op jit(solution)/shard_map/ppermute | solution.py:270
  328.1 23.5 %collective-permute-start.34 = (bf16[4,96,768]{2,1,0:T(8,128)(2,1)S(1)}, bf16[4,96,768]{2,1,0:T(8,128)(2,1)S(1)}, u32[]{:S(2)}, u32[]{:S(2)}) collective-permute-start(bf16[4,96,768]{2,1,0:T(8,128)(2,1)S(1)} %dynamic-slice_bitcast_fusion.5), channel_id=1, source_target_pairs={{0,2},{2,0},{4,6},{6,4},{8,10},{10,8},{12,14},{14,12},{1,3},{3,1},... | collective-permute-start | bytes 1769480 | tf_op jit(solution)/shard_map/ppermute | solution.py:270
  329.0 24.3 %collective-permute-start.54 = (bf16[96,1536]{1,0:T(8,128)(2,1)S(1)}, bf16[96,1536]{1,0:T(8,128)(2,1)S(1)}, u32[]{:S(2)}, u32[]{:S(2)}) collective-permute-start(bf16[96,1536]{1,0:T(8,128)(2,1)S(1)} %fusion.101), channel_id=1, source_target_pairs={{0,16},{16,0},{1,17},{17,1},{2,18},{18,2},{3,19},{19,3},{4,20},{20... | collective-permute-start | bytes 884744 | tf_op jit(solution)/shard_map/ppermute | solution.py:208
  343.2 95.6 %collective-permute-start.9 = (bf16[512,768]{1,0:T(8,128)(2,1)S(1)}, bf16[512,768]{1,0:T(8,128)(2,1)S(1)}, u32[]{:S(2)}, u32[]{:S(2)}) collective-permute-start(bf16[512,768]{1,0:T(8,128)(2,1)S(1)} %add_convert_fusion.5), channel_id=1, source_target_pairs={{0,1},{1,0},{2,3},{3,2},{4,5},{5,4},{6,7},{7,6},{8,9},{9,8},{10,11... | collective-permute-start | bytes 2359304 | tf_op jit(solution)/shard_map/ppermute | solution.py:208
  349.5 7.6 %collective-permute-start.43 = (bf16[96,768]{1,0:T(8,128)(2,1)S(1)}, bf16[96,768]{1,0:T(8,128)(2,1)S(1)}, u32[]{:S(2)}, u32[]{:S(2)}) collective-permute-start(bf16[96,768]{1,0:T(8,128)(2,1)S(1)} %get-tuple-element.135), channel_id=1, source_target_pairs={{0,12},{2,14},{4,0},{6,2},{8,4},{10,6},{12,8},{14,10},{1,13},{3,15... | collective-permute-start | bytes 442376 | tf_op jit(solution)/shard_map/ppermute | solution.py:285
  351.6 13.9 %collective-permute-start.42 = (bf16[96,768]{1,0:T(8,128)(2,1)S(1)}, bf16[96,768]{1,0:T(8,128)(2,1)S(1)}, u32[]{:S(2)}, u32[]{:S(2)}) collective-permute-start(bf16[96,768]{1,0:T(8,128)(2,1)S(1)} %get-tuple-element.136), channel_id=1, source_target_pairs={{0,8},{2,10},{4,12},{6,14},{8,0},{10,2},{12,4},{14,6},{1,9},{3,11}... | collective-permute-start | bytes 442376 | tf_op jit(solution)/shard_map/ppermute | solution.py:285
  353.3 12.2 %collective-permute-start.41 = (bf16[96,768]{1,0:T(8,128)(2,1)S(1)}, bf16[96,768]{1,0:T(8,128)(2,1)S(1)}, u32[]{:S(2)}, u32[]{:S(2)}) collective-permute-start(bf16[96,768]{1,0:T(8,128)(2,1)S(1)} %get-tuple-element.134), channel_id=1, source_target_pairs={{0,4},{2,6},{4,8},{6,10},{8,12},{10,14},{12,0},{14,2},{1,5},{3,7},... | collective-permute-start | bytes 442376 | tf_op jit(solution)/shard_map/ppermute | solution.py:285
  357.0 14.4 %collective-permute-start.37 = (bf16[96,768]{1,0:T(8,128)(2,1)S(1)}, bf16[96,768]{1,0:T(8,128)(2,1)S(1)}, u32[]{:S(2)}, u32[]{:S(2)}) collective-permute-start(bf16[96,768]{1,0:T(8,128)(2,1)S(1)} %get-tuple-element.132), channel_id=1, source_target_pairs={{0,12},{2,14},{4,0},{6,2},{8,4},{10,6},{12,8},{14,10},{1,13},{3,15... | collective-permute-start | bytes 442376 | tf_op jit(solution)/shard_map/ppermute | solution.py:285
  365.4 11.6 %collective-permute-start.36 = (bf16[96,768]{1,0:T(8,128)(2,1)S(1)}, bf16[96,768]{1,0:T(8,128)(2,1)S(1)}, u32[]{:S(2)}, u32[]{:S(2)}) collective-permute-start(bf16[96,768]{1,0:T(8,128)(2,1)S(1)} %get-tuple-element.133), channel_id=1, source_target_pairs={{0,8},{2,10},{4,12},{6,14},{8,0},{10,2},{12,4},{14,6},{1,9},{3,11}... | collective-permute-start | bytes 442376 | tf_op jit(solution)/shard_map/ppermute | solution.py:285
  365.5 13.3 %collective-permute-start.35 = (bf16[96,768]{1,0:T(8,128)(2,1)S(1)}, bf16[96,768]{1,0:T(8,128)(2,1)S(1)}, u32[]{:S(2)}, u32[]{:S(2)}) collective-permute-start(bf16[96,768]{1,0:T(8,128)(2,1)S(1)} %get-tuple-element.131), channel_id=1, source_target_pairs={{0,4},{2,6},{4,8},{6,10},{8,12},{10,14},{12,0},{14,2},{1,5},{3,7},... | collective-permute-start | bytes 442376 | tf_op jit(solution)/shard_map/ppermute | solution.py:285
  371.5 124.5 %collective-permute-start.27 = (bf16[768,768]{1,0:T(8,128)(2,1)}, bf16[768,768]{1,0:T(8,128)(2,1)}, u32[]{:S(2)}, u32[]{:S(2)}) collective-permute-start(bf16[768,768]{1,0:T(8,128)(2,1)} %constant_dynamic-slice_fusion.3), channel_id=1, source_target_pairs={{0,16},{16,0},{1,17},{17,1},{2,18},{18,2},{3,19},{19,3},{4,20},{20... | collective-permute-start | bytes 3538952 | tf_op jit(solution)/shard_map/ppermute | solution.py:270
  377.1 120.7 %collective-permute-start.21 = (bf16[768,768]{1,0:T(8,128)(2,1)}, bf16[768,768]{1,0:T(8,128)(2,1)}, u32[]{:S(2)}, u32[]{:S(2)}) collective-permute-start(bf16[768,768]{1,0:T(8,128)(2,1)} %constant_dynamic-slice_fusion.4), channel_id=1, source_target_pairs={{0,16},{16,0},{1,17},{17,1},{2,18},{18,2},{3,19},{19,3},{4,20},{20... | collective-permute-start | bytes 3538952 | tf_op jit(solution)/shard_map/ppermute | solution.py:270
  378.7 49.0 %collective-permute-start.44 = (bf16[96,768]{1,0:T(8,128)(2,1)S(1)}, bf16[96,768]{1,0:T(8,128)(2,1)S(1)}, u32[]{:S(2)}, u32[]{:S(2)}) collective-permute-start(bf16[96,768]{1,0:T(8,128)(2,1)S(1)} %fusion.154), channel_id=1, source_target_pairs={{0,16},{16,0},{1,17},{17,1},{2,18},{18,2},{3,19},{19,3},{4,20},{20... | collective-permute-start | bytes 442376 | tf_op jit(solution)/shard_map/ppermute | solution.py:208
  434.2 26.9 %collective-permute-start.19 = (bf16[96,1664]{1,0:T(8,128)(2,1)S(1)}, bf16[96,1664]{1,0:T(8,128)(2,1)S(1)}, u32[]{:S(2)}, u32[]{:S(2)}) collective-permute-start(bf16[96,1664]{1,0:T(8,128)(2,1)S(1)} %get-tuple-element.110), channel_id=1, source_target_pairs={{0,12},{2,14},{4,0},{6,2},{8,4},{10,6},{12,8},{14,10},{1,13},{3,15... | collective-permute-start | bytes 958472 | tf_op jit(solution)/shard_map/ppermute | solution.py:285
  434.3 30.2 %collective-permute-start.18 = (bf16[96,1664]{1,0:T(8,128)(2,1)S(1)}, bf16[96,1664]{1,0:T(8,128)(2,1)S(1)}, u32[]{:S(2)}, u32[]{:S(2)}) collective-permute-start(bf16[96,1664]{1,0:T(8,128)(2,1)S(1)} %get-tuple-element.111), channel_id=1, source_target_pairs={{0,8},{2,10},{4,12},{6,14},{8,0},{10,2},{12,4},{14,6},{1,9},{3,11}... | collective-permute-start | bytes 958472 | tf_op jit(solution)/shard_map/ppermute | solution.py:285
  438.8 25.6 %collective-permute-start.17 = (bf16[96,1664]{1,0:T(8,128)(2,1)S(1)}, bf16[96,1664]{1,0:T(8,128)(2,1)S(1)}, u32[]{:S(2)}, u32[]{:S(2)}) collective-permute-start(bf16[96,1664]{1,0:T(8,128)(2,1)S(1)} %get-tuple-element.109), channel_id=1, source_target_pairs={{0,4},{2,6},{4,8},{6,10},{8,12},{10,14},{12,0},{14,2},{1,5},{3,7},... | collective-permute-start | bytes 958472 | tf_op jit(solution)/shard_map/ppermute | solution.py:285
  461.1 29.2 %collective-permute-start.45 = (bf16[4,96,1536]{2,1,0:T(8,128)(2,1)}, bf16[4,96,1536]{2,1,0:T(8,128)(2,1)}, u32[]{:S(2)}, u32[]{:S(2)}) collective-permute-start(bf16[4,96,1536]{2,1,0:T(8,128)(2,1)} %dynamic-slice_bitcast_fusion.2), channel_id=1, source_target_pairs={{0,2},{2,0},{4,6},{6,4},{8,10},{10,8},{12,14},{14,12},{1,3},{3,1},... | collective-permute-start | bytes 3538952 | tf_op jit(solution)/shard_map/ppermute | solution.py:270
  464.5 51.5 %collective-permute-start.10 = (bf16[512,768]{1,0:T(8,128)(2,1)S(1)}, bf16[512,768]{1,0:T(8,128)(2,1)}, u32[]{:S(2)}, u32[]{:S(2)}) collective-permute-start(bf16[512,768]{1,0:T(8,128)(2,1)S(1)} %add_convert_fusion.4), channel_id=1, source_target_pairs={{0,1},{1,0},{2,3},{3,2},{4,5},{5,4},{6,7},{7,6},{8,9},{9,8},{10,11... | collective-permute-start | bytes 2359304 | tf_op jit(solution)/shard_map/ppermute | solution.py:208
  464.6 10.1 %collective-permute-start.20 = (bf16[96,1664]{1,0:T(8,128)(2,1)S(1)}, bf16[96,1664]{1,0:T(8,128)(2,1)}, u32[]{:S(2)}, u32[]{:S(2)}) collective-permute-start(bf16[96,1664]{1,0:T(8,128)(2,1)S(1)} %fusion.98), channel_id=1, source_target_pairs={{0,16},{16,0},{1,17},{17,1},{2,18},{18,2},{3,19},{19,3},{4,20},{20... | collective-permute-start | bytes 958472 | tf_op jit(solution)/shard_map/ppermute | solution.py:208
  474.8 165.0 %collective-permute-start.11 = (bf16[4,96,1536]{2,1,0:T(8,128)(2,1)}, bf16[4,96,1536]{2,1,0:T(8,128)(2,1)}, u32[]{:S(2)}, u32[]{:S(2)}) collective-permute-start(bf16[4,96,1536]{2,1,0:T(8,128)(2,1)} %dynamic-slice_bitcast_fusion.3), channel_id=1, source_target_pairs={{0,2},{2,0},{4,6},{6,4},{8,10},{10,8},{12,14},{14,12},{1,3},{3,1},... | collective-permute-start | bytes 3538952 | tf_op jit(solution)/shard_map/ppermute | solution.py:270
  492.1 10.7 %collective-permute-start.48 = (bf16[96,1536]{1,0:T(8,128)(2,1)S(1)}, bf16[96,1536]{1,0:T(8,128)(2,1)S(1)}, u32[]{:S(2)}, u32[]{:S(2)}) collective-permute-start(bf16[96,1536]{1,0:T(8,128)(2,1)S(1)} %get-tuple-element.113), channel_id=1, source_target_pairs={{0,12},{2,14},{4,0},{6,2},{8,4},{10,6},{12,8},{14,10},{1,13},{3,15... | collective-permute-start | bytes 884744 | tf_op jit(solution)/shard_map/ppermute | solution.py:285
  496.0 17.1 %collective-permute-start.47 = (bf16[96,1536]{1,0:T(8,128)(2,1)S(1)}, bf16[96,1536]{1,0:T(8,128)(2,1)S(1)}, u32[]{:S(2)}, u32[]{:S(2)}) collective-permute-start(bf16[96,1536]{1,0:T(8,128)(2,1)S(1)} %get-tuple-element.114), channel_id=1, source_target_pairs={{0,8},{2,10},{4,12},{6,14},{8,0},{10,2},{12,4},{14,6},{1,9},{3,11}... | collective-permute-start | bytes 884744 | tf_op jit(solution)/shard_map/ppermute | solution.py:285
  497.7 16.2 %collective-permute-start.46 = (bf16[96,1536]{1,0:T(8,128)(2,1)S(1)}, bf16[96,1536]{1,0:T(8,128)(2,1)S(1)}, u32[]{:S(2)}, u32[]{:S(2)}) collective-permute-start(bf16[96,1536]{1,0:T(8,128)(2,1)S(1)} %get-tuple-element.112), channel_id=1, source_target_pairs={{0,4},{2,6},{4,8},{6,10},{8,12},{10,14},{12,0},{14,2},{1,5},{3,7},... | collective-permute-start | bytes 884744 | tf_op jit(solution)/shard_map/ppermute | solution.py:285
  502.9 108.3 %collective-permute-start.28 = (bf16[4,96,768]{2,1,0:T(8,128)(2,1)}, bf16[4,96,768]{2,1,0:T(8,128)(2,1)}, u32[]{:S(2)}, u32[]{:S(2)}) collective-permute-start(bf16[4,96,768]{2,1,0:T(8,128)(2,1)} %dynamic-slice_bitcast_fusion.6), channel_id=1, source_target_pairs={{0,2},{2,0},{4,6},{6,4},{8,10},{10,8},{12,14},{14,12},{1,3},{3,1},... | collective-permute-start | bytes 1769480 | tf_op jit(solution)/shard_map/ppermute | solution.py:270
  513.0 101.6 %collective-permute-start.22 = (bf16[4,96,768]{2,1,0:T(8,128)(2,1)}, bf16[4,96,768]{2,1,0:T(8,128)(2,1)}, u32[]{:S(2)}, u32[]{:S(2)}) collective-permute-start(bf16[4,96,768]{2,1,0:T(8,128)(2,1)} %dynamic-slice_bitcast_fusion.7), channel_id=1, source_target_pairs={{0,2},{2,0},{4,6},{6,4},{8,10},{10,8},{12,14},{14,12},{1,3},{3,1},... | collective-permute-start | bytes 1769480 | tf_op jit(solution)/shard_map/ppermute | solution.py:270
  514.2 94.8 %collective-permute-start.49 = (bf16[96,1536]{1,0:T(8,128)(2,1)S(1)}, bf16[96,1536]{1,0:T(8,128)(2,1)}, u32[]{:S(2)}, u32[]{:S(2)}) collective-permute-start(bf16[96,1536]{1,0:T(8,128)(2,1)S(1)} %fusion.104), channel_id=1, source_target_pairs={{0,16},{16,0},{1,17},{17,1},{2,18},{18,2},{3,19},{19,3},{4,20},{20... | collective-permute-start | bytes 884744 | tf_op jit(solution)/shard_map/ppermute | solution.py:208
  612.5 7.6 %collective-permute-start.31 = (bf16[96,768]{1,0:T(8,128)(2,1)S(1)}, bf16[96,768]{1,0:T(8,128)(2,1)S(1)}, u32[]{:S(2)}, u32[]{:S(2)}) collective-permute-start(bf16[96,768]{1,0:T(8,128)(2,1)S(1)} %get-tuple-element.129), channel_id=1, source_target_pairs={{0,12},{2,14},{4,0},{6,2},{8,4},{10,6},{12,8},{14,10},{1,13},{3,15... | collective-permute-start | bytes 442376 | tf_op jit(solution)/shard_map/ppermute | solution.py:285
  612.6 15.0 %collective-permute-start.30 = (bf16[96,768]{1,0:T(8,128)(2,1)S(1)}, bf16[96,768]{1,0:T(8,128)(2,1)S(1)}, u32[]{:S(2)}, u32[]{:S(2)}) collective-permute-start(bf16[96,768]{1,0:T(8,128)(2,1)S(1)} %get-tuple-element.130), channel_id=1, source_target_pairs={{0,8},{2,10},{4,12},{6,14},{8,0},{10,2},{12,4},{14,6},{1,9},{3,11}... | collective-permute-start | bytes 442376 | tf_op jit(solution)/shard_map/ppermute | solution.py:285
  612.7 16.3 %collective-permute-start.29 = (bf16[96,768]{1,0:T(8,128)(2,1)S(1)}, bf16[96,768]{1,0:T(8,128)(2,1)S(1)}, u32[]{:S(2)}, u32[]{:S(2)}) collective-permute-start(bf16[96,768]{1,0:T(8,128)(2,1)S(1)} %get-tuple-element.128), channel_id=1, source_target_pairs={{0,4},{2,6},{4,8},{6,10},{8,12},{10,14},{12,0},{14,2},{1,5},{3,7},... | collective-permute-start | bytes 442376 | tf_op jit(solution)/shard_map/ppermute | solution.py:285
  615.9 15.3 %collective-permute-start.25 = (bf16[96,768]{1,0:T(8,128)(2,1)S(1)}, bf16[96,768]{1,0:T(8,128)(2,1)S(1)}, u32[]{:S(2)}, u32[]{:S(2)}) collective-permute-start(bf16[96,768]{1,0:T(8,128)(2,1)S(1)} %get-tuple-element.126), channel_id=1, source_target_pairs={{0,12},{2,14},{4,0},{6,2},{8,4},{10,6},{12,8},{14,10},{1,13},{3,15... | collective-permute-start | bytes 442376 | tf_op jit(solution)/shard_map/ppermute | solution.py:285
  620.2 18.4 %collective-permute-start.24 = (bf16[96,768]{1,0:T(8,128)(2,1)S(1)}, bf16[96,768]{1,0:T(8,128)(2,1)S(1)}, u32[]{:S(2)}, u32[]{:S(2)}) collective-permute-start(bf16[96,768]{1,0:T(8,128)(2,1)S(1)} %get-tuple-element.127), channel_id=1, source_target_pairs={{0,8},{2,10},{4,12},{6,14},{8,0},{10,2},{12,4},{14,6},{1,9},{3,11}... | collective-permute-start | bytes 442376 | tf_op jit(solution)/shard_map/ppermute | solution.py:285
  627.6 10.9 %collective-permute-start.23 = (bf16[96,768]{1,0:T(8,128)(2,1)S(1)}, bf16[96,768]{1,0:T(8,128)(2,1)S(1)}, u32[]{:S(2)}, u32[]{:S(2)}) collective-permute-start(bf16[96,768]{1,0:T(8,128)(2,1)S(1)} %get-tuple-element.125), channel_id=1, source_target_pairs={{0,4},{2,6},{4,8},{6,10},{8,12},{10,14},{12,0},{14,2},{1,5},{3,7},... | collective-permute-start | bytes 442376 | tf_op jit(solution)/shard_map/ppermute | solution.py:285
  629.1 17.4 %collective-permute-start.32 = (bf16[96,768]{1,0:T(8,128)(2,1)S(1)}, bf16[96,768]{1,0:T(8,128)(2,1)S(1)}, u32[]{:S(2)}, u32[]{:S(2)}) collective-permute-start(bf16[96,768]{1,0:T(8,128)(2,1)S(1)} %fusion.160), channel_id=1, source_target_pairs={{0,16},{16,0},{1,17},{17,1},{2,18},{18,2},{3,19},{19,3},{4,20},{20... | collective-permute-start | bytes 442376 | tf_op jit(solution)/shard_map/ppermute | solution.py:208
  638.6 7.9 %collective-permute-start.26 = (bf16[96,768]{1,0:T(8,128)(2,1)S(1)}, bf16[96,768]{1,0:T(8,128)(2,1)S(1)}, u32[]{:S(2)}, u32[]{:S(2)}) collective-permute-start(bf16[96,768]{1,0:T(8,128)(2,1)S(1)} %fusion.163), channel_id=1, source_target_pairs={{0,16},{16,0},{1,17},{17,1},{2,18},{18,2},{3,19},{19,3},{4,20},{20... | collective-permute-start | bytes 442376 | tf_op jit(solution)/shard_map/ppermute | solution.py:208
  642.4 16.2 %collective-permute-start.13 = (bf16[96,1536]{1,0:T(8,128)(2,1)S(1)}, bf16[96,1536]{1,0:T(8,128)(2,1)S(1)}, u32[]{:S(2)}, u32[]{:S(2)}) collective-permute-start(bf16[96,1536]{1,0:T(8,128)(2,1)S(1)} %get-tuple-element.120), channel_id=1, source_target_pairs={{0,8},{2,10},{4,12},{6,14},{8,0},{10,2},{12,4},{14,6},{1,9},{3,11}... | collective-permute-start | bytes 884744 | tf_op jit(solution)/shard_map/ppermute | solution.py:285
  644.5 14.1 %collective-permute-start.12 = (bf16[96,1536]{1,0:T(8,128)(2,1)S(1)}, bf16[96,1536]{1,0:T(8,128)(2,1)S(1)}, u32[]{:S(2)}, u32[]{:S(2)}) collective-permute-start(bf16[96,1536]{1,0:T(8,128)(2,1)S(1)} %get-tuple-element.118), channel_id=1, source_target_pairs={{0,4},{2,6},{4,8},{6,10},{8,12},{10,14},{12,0},{14,2},{1,5},{3,7},... | collective-permute-start | bytes 884744 | tf_op jit(solution)/shard_map/ppermute | solution.py:285
  (121 other events, 1159.0 us)
Sparse Core Ops, SparseCore 0:
  174.0 57.7 reduce-scatter.1

commit v2 on v1

--- a/solution.py
+++ b/solution.py
@@ -1,5 +1,4 @@
 import functools
-import math
 
 import jax
 import jax.numpy as jnp
@@ -307,6 +306,334 @@
     return jnp.concatenate([first, last], axis=1).astype(f32)
 
 
+def mesh_id(stream, batch):
+    return {"stream": stream, "batch": batch}
+
+
+def send(source, target, send_sem, recv_sem, device):
+    copy = pltpu.make_async_remote_copy(
+        src_ref=source,
+        dst_ref=target,
+        send_sem=send_sem,
+        recv_sem=recv_sem,
+        device_id=device,
+        device_id_type=pl.DeviceIdType.MESH,
+    )
+    copy.start()
+
+
+def await_send(source, send_sem):
+    pltpu.make_async_copy(source, source, send_sem).wait()
+
+
+def split_dot(contract, left, right):
+    high = left.astype(bf16)
+    low = (left - high.astype(f32)).astype(bf16)
+    return contract(high, right) + contract(low, right)
+
+
+def score_kernel(
+    count,
+    vectors,
+    doc_row,
+    top_mask,
+    positive,
+    grad,
+    loss,
+    queries,
+    docs,
+    raised,
+    totals,
+    logits,
+    stats,
+    own_loss,
+    other_loss,
+    sent_grads,
+    got_grads,
+    doc_sum,
+    sent_docs,
+    got_docs,
+    core_sent,
+    core_got,
+    query_send,
+    query_recv,
+    doc_send,
+    doc_recv,
+    stat_send,
+    stat_recv,
+    loss_sems,
+    grad_send,
+    grad_recv,
+    back_sems,
+    core_sems,
+):
+    side, batch, half = lax.axis_index("stream"), lax.axis_index("batch"), lax.axis_index("mp")
+    length, width = vectors.shape
+    quarter = length // 4
+    slots = quarter // QLEN
+    core = {"mp": 1 - half}
+    other = {"stream": 1 - side}
+    mine = side * count + batch
+
+    barrier = pltpu.get_barrier_semaphore()
+
+    def greet(step, carry):
+        peer = lax.rem(mine + step, 2 * count)
+        pl.semaphore_signal(
+            barrier,
+            inc=1,
+            device_id=mesh_id(peer // count, lax.rem(peer, count)),
+            device_id_type=pl.DeviceIdType.MESH,
+        )
+        return carry
+
+    lax.fori_loop(1, 2 * count, greet, 0)
+    pl.semaphore_signal(barrier, inc=1, device_id=core, device_id_type=pl.DeviceIdType.MESH)
+    pl.semaphore_wait(barrier, 2 * count)
+
+    def query_part(plane):
+        return vectors.at[pl.ds(pl.multiple_of(half * (length // 2), QLEN) + plane * quarter, quarter), :]
+
+    @pl.when(side == 0)
+    def _():
+        def push(step, carry):
+            peer = lax.rem(batch + step, count)
+            send(query_part(1), queries.at[batch], query_send.at[1, peer], query_recv.at[batch], mesh_id(1, peer))
+
+            @pl.when(step > 0)
+            def _():
+                send(query_part(0), queries.at[batch], query_send.at[0, peer], query_recv.at[batch], mesh_id(0, peer))
+
+            return carry
+
+        lax.fori_loop(0, count, push, 0)
+        queries[batch] = vectors[pl.ds(pl.multiple_of(half * (length // 2), QLEN), quarter), :]
+
+    @pl.when(side == 1)
+    def _():
+        send(vectors, docs, doc_send, doc_recv, mesh_id(0, batch))
+        docs[...] = vectors[...]
+
+    lane = lax.broadcasted_iota(jnp.int32, (width, length), 0)
+    onehot = jnp.where(lane == jnp.broadcast_to(doc_row[0:1, :], (width, length)), 1.0, 0.0).astype(bf16)
+
+    @pl.when(side == 0)
+    def _():
+        pltpu.make_async_copy(docs, docs, doc_recv).wait()
+
+    def await_queries(source):
+        @pl.when(jnp.logical_or(side == 1, source != batch))
+        def _():
+            pltpu.make_async_copy(queries.at[source], queries.at[source], query_recv.at[source]).wait()
+
+    def forward(step, carry):
+        source = lax.rem(batch + step, count)
+        await_queries(source)
+        sims = dot_nt(queries[source], docs[...]) * (1.0 / temper)
+        for slot in range(slots):
+            chosen = top_mask[pl.ds(source * 2 * slots + side * slots + slot, 1), :].astype(f32)
+            part = jnp.exp(sims[slot * QLEN : (slot + 1) * QLEN]) * chosen
+            raised[source, slot * QLEN : (slot + 1) * QLEN, :] = part
+        summed = split_dot(dot_nt, raised[source], onehot)
+        totals[source] = summed
+        pooled = jnp.log1p(summed) * (logit_scale * temper / QLEN)
+        for slot in range(slots):
+            logits[pl.ds(source * slots + slot, 1), :] = jnp.sum(
+                pooled[slot * QLEN : (slot + 1) * QLEN], axis=0, keepdims=True
+            )
+        return carry
+
+    lax.fori_loop(0, count, forward, 0)
+
+    doc = lax.broadcasted_iota(jnp.int32, logits.shape, 1)
+    local = doc < DOCS_ROW
+    scores = logits[...]
+    is_positive = jnp.where(
+        jnp.logical_and(local, positive[...] == doc + batch * DOCS_ROW), 1.0, 0.0
+    )
+    exps = jnp.sum(jnp.where(local, jnp.exp(scores), 0.0), axis=1, keepdims=True)
+    hits = jnp.sum(is_positive * scores, axis=1, keepdims=True)
+    stats[batch] = jnp.where(doc == 0, exps, jnp.where(doc == 1, hits, 0.0))
+
+    def push_stats(step, carry):
+        peer = lax.rem(batch + step, count)
+        send(stats.at[batch], stats.at[batch], stat_send.at[peer], stat_recv.at[batch], mesh_id(side, peer))
+        return carry
+
+    lax.fori_loop(1, count, push_stats, 0)
+
+    def take_stats(step, carry):
+        peer = lax.rem(batch + step, count)
+        pltpu.make_async_copy(stats.at[peer], stats.at[peer], stat_recv.at[peer]).wait()
+        return carry
+
+    lax.fori_loop(1, count, take_stats, 0)
+    summed = lax.fori_loop(1, count, lambda source, total: total + stats[source], stats[0])
+    log_total = jnp.log(jnp.sum(jnp.where(doc == 0, summed, 0.0), axis=1, keepdims=True))
+    hit_total = jnp.sum(jnp.where(doc == 1, summed, 0.0), axis=1, keepdims=True)
+    losses = jnp.broadcast_to(log_total - hit_total, logits.shape)
+    sent_grad = jnp.where(local, jnp.exp(scores - log_total), 0.0) - is_positive
+    logits[...] = losses
+    for slot in range(slots):
+        own_loss[pl.ds(slot, 1), :] = logits[pl.ds(batch * slots + slot, 1), :]
+    send(own_loss, other_loss, loss_sems.at[0], loss_sems.at[1], other)
+    logits[...] = sent_grad
+    doc_sum[...] = jnp.zeros(doc_sum.shape, f32)
+
+    def backward(step, carry):
+        source = lax.rem(batch + step + 1, count)
+        parts = []
+        for slot in range(slots):
+            line = logits[pl.ds(source * slots + slot, 1), :] * (logit_scale / QLEN)
+            parts.append(line / (1.0 + totals[source, slot * QLEN : (slot + 1) * QLEN, :]))
+        spread = split_dot(dot, jnp.concatenate(parts, axis=0), onehot)
+        ds = (raised[source] * spread).astype(bf16)
+        back = dot(ds, docs[...]).astype(bf16)
+        doc_sum[...] += dot_tn(ds, queries[source])
+
+        @pl.when(jnp.logical_or(side == 1, source != batch))
+        def _():
+            sent_grads[source] = back
+            send(
+                sent_grads.at[source],
+                got_grads.at[side, batch],
+                grad_send.at[source],
+                grad_recv.at[side, batch],
+                mesh_id(0, source),
+            )
+
+        @pl.when(jnp.logical_and(side == 0, source == batch))
+        def _():
+            got_grads[0, batch] = back
+
+        return carry
+
+    lax.fori_loop(0, count, backward, 0)
+
+    @pl.when(side == 0)
+    def _():
+        sent_docs[...] = doc_sum[...].astype(bf16)
+        send(sent_docs, got_docs, back_sems.at[0], back_sems.at[1], mesh_id(1, batch))
+
+        def take(step, carry):
+            peer = lax.rem(batch + step, count)
+
+            @pl.when(step > 0)
+            def _():
+                pltpu.make_async_copy(got_grads.at[0, peer], got_grads.at[0, peer], grad_recv.at[0, peer]).wait()
+
+            pltpu.make_async_copy(got_grads.at[1, peer], got_grads.at[1, peer], grad_recv.at[1, peer]).wait()
+            return carry
+
+        lax.fori_loop(0, count, take, 0)
+        for plane in range(2):
+            total = lax.fori_loop(
+                1,
+                count,
+                lambda source, total, plane=plane: total + got_grads[plane, source].astype(f32),
+                got_grads[plane, 0].astype(f32),
+            )
+            core_sent[plane * quarter : (plane + 1) * quarter, :] = total.astype(bf16)
+        part = core_sent.at[pl.ds(0, length // 2), :]
+        there = core_got.at[pl.ds(0, length // 2), :]
+        send(part, there, core_sems.at[0], core_sems.at[1], core)
+        pltpu.make_async_copy(there, there, core_sems.at[1]).wait()
+        first = pl.multiple_of(half * (length // 2), QLEN)
+        grad[pl.ds(first, length // 2), :] = core_sent[pl.ds(0, length // 2), :].astype(f32)
+        grad[pl.ds(length // 2 - first, length // 2), :] = core_got[pl.ds(0, length // 2), :].astype(f32)
+        await_send(part, core_sems.at[0])
+        await_send(sent_docs, back_sems.at[0])
+
+    @pl.when(side == 1)
+    def _():
+        pltpu.make_async_copy(got_docs, got_docs, back_sems.at[1]).wait()
+        core_sent[...] = (doc_sum[...] + got_docs[...].astype(f32)).astype(bf16)
+        send(core_sent, core_got, core_sems.at[0], core_sems.at[1], core)
+        pltpu.make_async_copy(core_got, core_got, core_sems.at[1]).wait()
+        grad[...] = (core_sent[...].astype(f32) + core_got[...].astype(f32)).astype(bf16).astype(f32)
+        await_send(core_sent, core_sems.at[0])
+        await_send(vectors, doc_send)
+
+    pltpu.make_async_copy(other_loss, other_loss, loss_sems.at[1]).wait()
+    lower = jnp.where(side == 0, own_loss[0:slots, :], other_loss[0:slots, :])
+    upper = jnp.where(side == 0, other_loss[0:slots, :], own_loss[0:slots, :])
+    loss[...] = jnp.concatenate([lower, upper], axis=0)
+    await_send(own_loss, loss_sems.at[0])
+
+    def settle(step, carry):
+        peer = lax.rem(batch + step, count)
+
+        @pl.when(step > 0)
+        def _():
+            await_send(stats.at[batch], stat_send.at[peer])
+
+        @pl.when(jnp.logical_or(side == 1, step > 0))
+        def _():
+            await_send(sent_grads.at[peer], grad_send.at[peer])
+
+        @pl.when(side == 0)
+        def _():
+            await_send(query_part(1), query_send.at[1, peer])
+
+            @pl.when(step > 0)
+            def _():
+                await_send(query_part(0), query_send.at[0, peer])
+
+        return carry
+
+    lax.fori_loop(0, count, settle, 0)
+
+
+def score(vectors, doc_row, top_mask, positive):
+    count = lax.axis_size("batch")
+    length, width = vectors.shape
+    quarter = length // 4
+    slots = quarter // QLEN
+    dma = pltpu.SemaphoreType.DMA
+    return pl.pallas_call(
+        functools.partial(score_kernel, count),
+        out_shape=(
+            jax.ShapeDtypeStruct((length, width), f32),
+            jax.ShapeDtypeStruct((2 * slots, width), f32),
+        ),
+        in_specs=[pl.BlockSpec(memory_space=pltpu.VMEM)] * 4,
+        out_specs=(pl.BlockSpec(memory_space=pltpu.VMEM),) * 2,
+        scratch_shapes=[
+            pltpu.VMEM((count, quarter, width), bf16),
+            pltpu.VMEM((length, width), bf16),
+            pltpu.VMEM((count, quarter, length), f32),
+            pltpu.VMEM((count, quarter, width), f32),
+            pltpu.VMEM((count * slots, width), f32),
+            pltpu.VMEM((count, count * slots, width), f32),
+            pltpu.VMEM((8, width), f32),
+            pltpu.VMEM((8, width), f32),
+            pltpu.VMEM((count, quarter, width), bf16),
+            pltpu.VMEM((2, count, quarter, width), bf16),
+            pltpu.VMEM((length, width), f32),
+            pltpu.VMEM((length, width), bf16),
+            pltpu.VMEM((length, width), bf16),
+            pltpu.VMEM((length, width), bf16),
+            pltpu.VMEM((length, width), bf16),
+            dma((2, count)),
+            dma((count,)),
+            dma,
+            dma,
+            dma((count,)),
+            dma((count,)),
+            dma((2,)),
+            dma((count,)),
+            dma((2, count)),
+            dma((2,)),
+            dma((2,)),
+        ],
+        compiler_params=pltpu.CompilerParams(
+            collective_id=0, has_side_effects=True, vmem_limit_bytes=56 * 1024 * 1024
+        ),
+        cost_estimate=pl.CostEstimate(flops=10**9, bytes_accessed=2 * 10**6, transcendentals=10**6),
+        name="score",
+    )(vectors, doc_row, top_mask, positive)
+
+
 def on_device(
     tokens,
     segments,
@@ -362,83 +689,16 @@
     unit_vectors, normalize_back = jax.vjp(normalize, projected)
     vectors = unit_vectors.astype(bf16)
     own_vectors = lax.dynamic_slice_in_dim(vectors, mp_index * share_len, share_len, 0)
-    sent_half = lax.ppermute(own_vectors, "stream", [(0, 1)])
-    gathered = lax.all_gather(sent_half, "batch", axis=0)
-    query_rows = gathered.shape[0]
-    per_half = share_len // QLEN
-    block_rows = math.gcd(query_rows, 8)
-    block_count = query_rows // block_rows
-    block_slots = block_rows * per_half
-    block_tokens = block_slots * QLEN
-    doc_tokens = length
-    query_blocks = gathered.reshape(block_count, block_tokens, -1)
-    mask_cols = jnp.transpose(top_mask.reshape(query_rows * per_half, doc_tokens), (1, 0)).astype(
-        f32
-    )
-    mask_blocks = jnp.transpose(mask_cols.reshape(doc_tokens, block_count, block_slots), (1, 0, 2))
-    doc_flat = vectors
-    local_docs = DOCS_ROW
-    doc_ids = segments.reshape(-1)
-    doc_onehot = (jnp.arange(local_docs, dtype=jnp.int32)[:, None] == doc_ids[None, :]).astype(f32)
-
-    def pooled_sums(query_block, mask_block):
-        similarity = dot_nt(doc_flat, query_block)
-        mask_wide = jnp.broadcast_to(
-            mask_block[:, :, None], (doc_tokens, block_slots, QLEN)
-        ).reshape(doc_tokens, block_tokens)
-        raised = jnp.exp(similarity / temper) * mask_wide
-        totals = jnp.einsum("nt,tk->nk", doc_onehot, raised, precision=highest)
-        return (raised, totals)
-
-    def block_logits(inputs):
-        raised, totals = pooled_sums(inputs[0], inputs[1])
-        pooled = jnp.mean(
-            (temper * jnp.log1p(totals)).reshape(local_docs, block_slots, QLEN), axis=-1
-        )
-        return logit_scale * pooled
-
-    logit_blocks = lax.map(block_logits, (query_blocks, mask_blocks))
-    logits = jnp.transpose(logit_blocks, (0, 2, 1)).reshape(query_rows, per_half, local_docs)
-    global_docs = batch_index * local_docs + jnp.arange(local_docs, dtype=jnp.int32)
-    is_positive = (global_docs[None, None, :] == positive[:, :, None]).astype(f32)
-    doc_side = stream_side == 1
-    stats = jnp.stack([jnp.sum(jnp.exp(logits), axis=-1), jnp.sum(logits * is_positive, axis=-1)])
-    stats = lax.psum(jnp.where(doc_side, stats, 0.0), ("stream", "batch"))
-    log_total = jnp.log(stats[0])
-    losses = log_total - stats[1]
-    query_loss = lax.dynamic_slice_in_dim(losses, batch_index * row_count, row_count, 0)
-    grad_logits = jnp.exp(logits - log_total[..., None]) - is_positive
-    grad_blocks = jnp.transpose(
-        grad_logits.reshape(block_count, block_slots, local_docs), (0, 2, 1)
-    )
-
-    def block_back(doc_grad, inputs):
-        query_block, mask_block, grad_block = inputs
-        raised, totals = pooled_sums(query_block, mask_block)
-        grad_wide = jnp.broadcast_to(
-            grad_block[:, :, None], (local_docs, block_slots, QLEN)
-        ).reshape(local_docs, block_tokens)
-        factor = grad_wide * (logit_scale / QLEN) / (1.0 + totals)
-        spread = jnp.einsum("nt,nk->tk", doc_onehot, factor, precision=highest)
-        grad_sims = (raised * spread).astype(bf16)
-        grad_block_query = dot_tn(grad_sims, doc_flat)
-        doc_grad = doc_grad + dot(grad_sims, query_block)
-        return (doc_grad, grad_block_query)
-
-    doc_grad, grad_query_blocks = lax.scan(
-        block_back, jnp.zeros(doc_flat.shape, f32), (query_blocks, mask_blocks, grad_blocks)
-    )
-    summed_query = lax.psum_scatter(
-        grad_query_blocks.reshape(query_rows, share_len, -1).astype(bf16),
-        "batch",
-        scatter_dimension=0,
-        tiled=False,
-    )
-    returned = lax.ppermute(summed_query, "stream", [(1, 0)])
-    returned = lax.all_gather(returned, "mp", axis=0, tiled=True)
-    grad_vectors = jnp.where(
-        stream_side == 0, returned.astype(f32), sum_of_two(doc_grad, "mp").astype(bf16).astype(f32)
-    )
+    query_rows, slot_count = positive.shape
+    plane_slots = slot_count // 2
+    own_slots = lax.dynamic_slice_in_dim(positive, stream_side * plane_slots, plane_slots, 1)
+    grad_vectors, losses = score(
+        vectors,
+        jnp.broadcast_to(segments, (8, length)),
+        top_mask.reshape(query_rows * slot_count, length),
+        jnp.broadcast_to(own_slots.reshape(-1, 1), (query_rows * plane_slots, vectors.shape[1])),
+    )
+    query_loss = losses[:, 0][None]
     grad_projected = normalize_back(grad_vectors)[0].astype(bf16)
     grad_proj = dot_tn(final_in, grad_projected).astype(bf16)
     grad_final = dot_nt(grad_projected, w_proj)

time: 679 us -> 549 us (0.81); the launches traced: 675 us -> 538 us
  blocking collectives: 167 us -> 89.6 us
  waiting for transfers between devices: 205 us -> 153 us
  Pallas kernels: 41.7 us -> 80 us
  starting transfers between devices: 67.6 us -> 53.8 us
  between operations: 16.2 us -> 2.68 us
  matrix products: 72.2 us -> 61.6 us
    reduce_scatter x1 -> x0, waiting for transfers between devices: 50.1 us -> none  [on_device(): lax.psum_scatter(grad_query_blocks.reshape(query_rows, share_len, -1).ast...]
    psum x1 -> x0, blocking collectives: 43 us -> none  [on_device(): stats = lax.psum(jnp.where(doc_side, stats, 0.0), ('stream', 'batch'))]
    pallas_call x0 -> x1, Pallas kernels: none -> 38.3 us  [score(): pl.pallas_call(functools.partial(score_kernel, count), out_shape=(jax.Sha...]
    all_gather x2 -> x0, blocking collectives: 34.4 us -> none  [the longest x1 32 us: on_device(): gathered = lax.all_gather(sent_half, 'batch', axis=0)]
    reshape x3 -> x0, local copies, waits for them, and re-layouts: 8.75 us -> none  [the longest x1 5.37 us: pooled_sums(): mask_wide = jnp.broadcast_to(mask_block[:, :, None], (doc_tokens, block_s...]
    unnamed x227 -> x183, local copies, waits for them, and re-layouts: 13.1 us -> 15.7 us
    dot_general x16 -> x15, matrix products: 31 us -> 29.1 us  [dot(): lax.dot_general(a, b, (((1,), (0,)), ((), ())), preferred_element_type=f32)]
    dot_general x16 -> x15, matrix products: 19 us -> 17.4 us  [dot_tn(): lax.dot_general(a, b, (((0,), (0,)), ((), ())), preferred_element_type=f32)]
  transfers between devices with their start and end apart: 56 -> 52, of which waited for: 25 -> 21; matrix products, arithmetic and copies ran while one was open for 15% -> 18% of each run, Pallas kernels for 4% -> 5%
where the time goes in v2:
time: 549 us; the launch traced here: 538 us
  waiting for transfers between devices  153 us (28%)
  blocking collectives  89.6 us (16%)
  Pallas kernels  80 us (15%)
  matrix products  61.6 us (11%)
  starting transfers between devices  53.8 us (10%)
  local copies, waits for them, and re-layouts  49.8 us (9%)
  other arithmetic  48.2 us (9%)
    psum x1, blocking collectives, on_device(): lax.psum((grad_bias_local, grad_gains), ('stream', 'batch'))  86.8 us
    ppermute x24, waiting for transfers between devices, scatter_outer(): lax.ppermute(pick(part, (outer + step) % count, 0), 'batch', pairs)  68 us
    ppermute x16, waiting for transfers between devices, swap(): return lax.ppermute(value, axis, [(0, 1), (1, 0)])  63.2 us
    pallas_call x1, Pallas kernels, score(): pl.pallas_call(functools.partial(score_kernel, count), out_shape=(jax.Sha...  38.3 us
    ppermute x24, starting transfers between devices, scatter_outer(): lax.ppermute(pick(part, (outer + step) % count, 0), 'batch', pairs)  32.5 us
    dot_general x15, matrix products, dot(): lax.dot_general(a, b, (((1,), (0,)), ((), ())), preferred_element_type=f32)  29.1 us
    pallas_call x2, Pallas kernels, attend_back(): pl.pallas_call(attend_back_kernel, out_shape=(grad, grad, grad, jax.Shape...  24.8 us
    ppermute x12, waiting for transfers between devices, paired(): lax.ppermute(sent, axis, pairs).astype(f32)  21.3 us
  transfers between devices with their start and end apart: 52, of which 21 were waited for; matrix products, arithmetic and copies ran while one was open for 18% of the time, Pallas kernels for 5%

profile of v2, /device:TPU:0, one launch (start us, length us, event | category | flops | bytes accessed | tf_op | source)
XLA Modules:
  0.0 538.3 jit_solution(17895146814156042144)
XLA Ops:
  0.7 2.8 all-gather
  10.2 8.5 %attend.2 = (bf16[512,384]{1,0:T(8,128)(2,1)S(1)}, f32[512,128]{1,0:T(8,128)S(1)}) custom-call(f32[8,512]{1,0:T(8,128)S(1)} %fusion.166.table, s32[8,512]{1,0:T(8,128)S(1)} %broadcast_in_dim.33.row_ids, s32[512,128]{1,0:T(8,128)S(1)} %broadcast_in_dim.34.col_ids, bf16[512,384]{1,0:T(8,128)(2,1)S(1)} %convolution_convert_fusion.23.q, ...), custom_call_target="tpu_custom_call" | custom-call | flops 1000000000 | bytes 3000000 | tf_op jit(solution)/shard_map/attend/pallas_call | solution.py:106
  19.8 1.9 collective-permute-done
  23.8 3.1 multiply_convert_fusion.3
  28.8 1.9 collective-permute-done.1
  34.9 8.5 %attend.3 = (bf16[512,384]{1,0:T(8,128)(2,1)S(1)}, f32[512,128]{1,0:T(8,128)S(1)}) custom-call(f32[8,512]{1,0:T(8,128)S(1)} %fusion.166.table, s32[8,512]{1,0:T(8,128)S(1)} %broadcast_in_dim.33.row_ids, s32[512,128]{1,0:T(8,128)S(1)} %broadcast_in_dim.34.col_ids, bf16[512,384]{1,0:T(8,128)(2,1)S(1)} %convolution_convert_fusion.20.q, ...), custom_call_target="tpu_custom_call" | custom-call | flops 1000000000 | bytes 3000000 | tf_op jit(solution)/shard_map/attend/pallas_call | solution.py:106
  44.4 1.9 collective-permute-done.2
  49.5 3.3 multiply_convert_fusion.2
  52.8 2.3 fusion.81
  59.8 2.5 convert_bitcast_fusion.1
  62.3 1.8 multiply_reduce_fusion.8
  65.2 1.8 multiply_reduce_fusion.13
  67.0 1.8 copy.36
  73.8 38.3 %score.1 = (f32[512,128]{1,0:T(8,128)}, f32[8,128]{1,0:T(8,128)}) custom-call(bf16[512,128]{1,0:T(8,128)(2,1)} %multiply_convert_fusion.8.vectors, s32[8,512]{1,0:T(8,128)} %broadcast_in_dim.36.doc_row, s32[64,512]{1,0:T(8,128)} %bitcast.380, s32[32,128]{1,0:T(8,128)} %broadcast_in_dim.38.positive), custom_call_target="tpu_custom_call" | custom-call | flops 1000000000 | bytes 2000000 | tf_op jit(solution)/shard_map/score/pallas_call | solution.py:593
  117.3 5.1 fusion.13
  142.5 12.6 %attend_back.2 = (bf16[512,384]{1,0:T(8,128)(2,1)S(1)}, bf16[512,384]{1,0:T(8,128)(2,1)S(1)}, bf16[512,384]{1,0:T(8,128)(2,1)S(1)}, f32[8,512]{1,0:T(8,128)S(1)}) custom-call(f32[8,512]{1,0:T(8,128)S(1)} %fusion.166.table, s32[8,512]{1,0:T(8,128)S(1)} %broadcast_in_dim.33.row_ids, s32[512,128]{1,0:T(8,128)S(1)} %broadcast_in_dim.34.col_ids, ...), custom_call_target="tpu_custom_call" | custom-call | flops 2500000000 | bytes 4000000 | tf_op jit(solution)/shard_map/attend_back/pallas_call | solution.py:176
  163.6 4.5 copy.40
  172.4 1.8 collective-permute-start.50
  176.5 6.9 %collective-permute-done.30 = bf16[768,768]{1,0:T(8,128)(2,1)} collective-permute-done((bf16[768,768]{1,0:T(8,128)(2,1)}, bf16[768,768]{1,0:T(8,128)(2,1)}, u32[]{:S(2)}, u32[]{:S(2)}) %collective-permute-start.30) | collective-permute-done | bytes 1179680 | tf_op jit(solution)/shard_map/ppermute | solution.py:269
  187.8 12.9 %collective-permute-done.49 = bf16[96,1536]{1,0:T(8,128)(2,1)S(1)} collective-permute-done((bf16[96,1536]{1,0:T(8,128)(2,1)S(1)}, bf16[96,1536]{1,0:T(8,128)(2,1)S(1)}, u32[]{:S(2)}, u32[]{:S(2)}) %collective-permute-start.49) | collective-permute-done | bytes 294944 | tf_op jit(solution)/shard_map/ppermute | solution.py:284
  205.6 5.1 fusion.6
  222.9 2.2 collective-permute-done.31
  226.3 1.8 collective-permute-start.38
  231.5 7.7 %collective-permute-done.39 = bf16[96,768]{1,0:T(8,128)(2,1)S(1)} collective-permute-done((bf16[96,768]{1,0:T(8,128)(2,1)S(1)}, bf16[96,768]{1,0:T(8,128)(2,1)S(1)}, u32[]{:S(2)}, u32[]{:S(2)}) %collective-permute-start.39) | collective-permute-done | bytes 147488 | tf_op jit(solution)/shard_map/ppermute | solution.py:284
  239.2 5.3 collective-permute-start.32
  246.3 4.2 collective-permute-done.33
  252.6 48.1 %collective-permute-done.41 = bf16[96,768]{1,0:T(8,128)(2,1)S(1)} collective-permute-done((bf16[96,768]{1,0:T(8,128)(2,1)S(1)}, bf16[96,768]{1,0:T(8,128)(2,1)S(1)}, u32[]{:S(2)}, u32[]{:S(2)}) %collective-permute-start.41) | collective-permute-done | bytes 147488 | tf_op jit(solution)/shard_map/ppermute | solution.py:207
  302.5 3.4 collective-permute-done.35
  307.3 4.3 collective-permute-start.15
  314.5 12.2 %attend_back.3 = (bf16[512,384]{1,0:T(8,128)(2,1)S(1)}, bf16[512,384]{1,0:T(8,128)(2,1)S(1)}, bf16[512,384]{1,0:T(8,128)(2,1)S(1)}, f32[8,512]{1,0:T(8,128)S(1)}) custom-call(f32[8,512]{1,0:T(8,128)S(1)} %fusion.166.table, s32[8,512]{1,0:T(8,128)S(1)} %broadcast_in_dim.33.row_ids, s32[512,128]{1,0:T(8,128)S(1)} %broadcast_in_dim.34.col_ids, ...), custom_call_target="tpu_custom_call" | custom-call | flops 2500000000 | bytes 4000000 | tf_op jit(solution)/shard_map/attend_back/pallas_call | solution.py:176
  334.7 2.3 collective-permute-done.15
  337.2 1.8 collective-permute-start.17
  339.1 4.3 copy.39
  343.5 2.4 dynamic-slice_bitcast_fusion.3
  350.9 12.2 %collective-permute-done.42 = bf16[4,96,1536]{2,1,0:T(8,128)(2,1)} collective-permute-done((bf16[4,96,1536]{2,1,0:T(8,128)(2,1)}, bf16[4,96,1536]{2,1,0:T(8,128)(2,1)}, u32[]{:S(2)}, u32[]{:S(2)}) %collective-permute-start.42) | collective-permute-done | bytes 1179680 | tf_op jit(solution)/shard_map/ppermute | solution.py:269
  364.9 3.9 collective-permute-start.45
  375.6 9.8 %collective-permute-done.44 = bf16[96,1536]{1,0:T(8,128)(2,1)S(1)} collective-permute-done((bf16[96,1536]{1,0:T(8,128)(2,1)S(1)}, bf16[96,1536]{1,0:T(8,128)(2,1)S(1)}, u32[]{:S(2)}, u32[]{:S(2)}) %collective-permute-start.44) | collective-permute-done | bytes 294944 | tf_op jit(solution)/shard_map/ppermute | solution.py:284
  388.0 3.0 fusion.61
  391.2 86.8 %all-reduce.1 = (f32[5,768]{1,0:T(8,128)S(1)}, f32[32,6]{0,1:T(8,128)}) all-reduce(f32[5,768]{1,0:T(8,128)S(1)} %stack.112, f32[32,6]{0,1:T(8,128)S(1)} %fusion.165), channel_id=1, replica_groups=mesh['stream'=2,'batch'=8,'mp'=2] {'stream','batch'}, use_global_device_ids=true, to_apply=%region_17.18 | all-reduce | flops 4032 | bytes 32256 | tf_op jit(solution)/shard_map/psum | solution.py:730
  478.6 2.5 fusion.94
  482.7 2.0 collective-permute-start.26
  485.9 2.4 collective-permute-start.22
  491.2 10.2 %collective-permute-done.27 = bf16[96,768]{1,0:T(8,128)(2,1)S(1)} collective-permute-done((bf16[96,768]{1,0:T(8,128)(2,1)S(1)}, bf16[96,768]{1,0:T(8,128)(2,1)S(1)}, u32[]{:S(2)}, u32[]{:S(2)}) %collective-permute-start.27) | collective-permute-done | bytes 147488 | tf_op jit(solution)/shard_map/ppermute | solution.py:284
  501.6 7.0 %collective-permute-done.21 = bf16[96,768]{1,0:T(8,128)(2,1)S(1)} collective-permute-done((bf16[96,768]{1,0:T(8,128)(2,1)S(1)}, bf16[96,768]{1,0:T(8,128)(2,1)S(1)}, u32[]{:S(2)}, u32[]{:S(2)}) %collective-permute-start.21) | collective-permute-done | bytes 147488 | tf_op jit(solution)/shard_map/ppermute | solution.py:284
  512.0 2.2 collective-permute-start.10
  514.2 1.9 collective-permute-start.9
  517.3 11.0 %collective-permute-done.10 = bf16[96,1536]{1,0:T(8,128)(2,1)S(1)} collective-permute-done((bf16[96,1536]{1,0:T(8,128)(2,1)S(1)}, bf16[96,1536]{1,0:T(8,128)(2,1)S(1)}, u32[]{:S(2)}, u32[]{:S(2)}) %collective-permute-start.10) | collective-permute-done | bytes 294944 | tf_op jit(solution)/shard_map/ppermute | solution.py:284
  530.8 4.5 collective-permute-done.12
  (413 shorter events, 146.9 us)
Async XLA Ops:
  55.1 7.1 %collective-permute-start.3 = (bf16[512,768]{1,0:T(8,128)(2,1)}, bf16[512,768]{1,0:T(8,128)(2,1)}, u32[]{:S(2)}, u32[]{:S(2)}) collective-permute-start(bf16[512,768]{1,0:T(8,128)(2,1)} %fusion.81), channel_id=1, source_target_pairs={{0,1},{1,0},{2,3},{3,2},{4,5},{5,4},{6,7},{7,6},{8,9},{9,8},{10,11... | collective-permute-start | bytes 2359304 | tf_op jit(solution)/shard_map/ppermute | solution.py:207
  128.2 10.3 %collective-permute-start.4 = (bf16[512,768]{1,0:T(8,128)(2,1)S(1)}, bf16[512,768]{1,0:T(8,128)(2,1)S(1)}, u32[]{:S(2)}, u32[]{:S(2)}) collective-permute-start(bf16[512,768]{1,0:T(8,128)(2,1)S(1)} %add_convert_fusion.7), channel_id=1, source_target_pairs={{0,1},{1,0},{2,3},{3,2},{4,5},{5,4},{6,7},{7,6},{8,9},{9,8},{10,11... | collective-permute-start | bytes 2359304 | tf_op jit(solution)/shard_map/ppermute | solution.py:207
  129.8 44.4 %collective-permute-start.36 = (bf16[768,768]{1,0:T(8,128)(2,1)}, bf16[768,768]{1,0:T(8,128)(2,1)}, u32[]{:S(2)}, u32[]{:S(2)}) collective-permute-start(bf16[768,768]{1,0:T(8,128)(2,1)} %constant_dynamic-slice_fusion.1), channel_id=1, source_target_pairs={{0,16},{16,0},{1,17},{17,1},{2,18},{18,2},{3,19},{19,3},{4,20},{20... | collective-permute-start | bytes 3538952 | tf_op jit(solution)/shard_map/ppermute | solution.py:269
  131.6 51.8 %collective-permute-start.30 = (bf16[768,768]{1,0:T(8,128)(2,1)}, bf16[768,768]{1,0:T(8,128)(2,1)}, u32[]{:S(2)}, u32[]{:S(2)}) collective-permute-start(bf16[768,768]{1,0:T(8,128)(2,1)} %constant_dynamic-slice_fusion.2), channel_id=1, source_target_pairs={{0,16},{16,0},{1,17},{17,1},{2,18},{18,2},{3,19},{19,3},{4,20},{20... | collective-permute-start | bytes 3538952 | tf_op jit(solution)/shard_map/ppermute | solution.py:269
  135.5 35.1 %collective-permute-start.47 = (bf16[4,96,1536]{2,1,0:T(8,128)(2,1)}, bf16[4,96,1536]{2,1,0:T(8,128)(2,1)}, u32[]{:S(2)}, u32[]{:S(2)}) collective-permute-start(bf16[4,96,1536]{2,1,0:T(8,128)(2,1)} %dynamic-slice_bitcast_fusion.1), channel_id=1, source_target_pairs={{0,2},{2,0},{4,6},{6,4},{8,10},{10,8},{12,14},{14,12},{1,3},{3,1},... | collective-permute-start | bytes 3538952 | tf_op jit(solution)/shard_map/ppermute | solution.py:269
  158.0 44.3 %collective-permute-start.5 = (bf16[512,768]{1,0:T(8,128)(2,1)S(1)}, bf16[512,768]{1,0:T(8,128)(2,1)S(1)}, u32[]{:S(2)}, u32[]{:S(2)}) collective-permute-start(bf16[512,768]{1,0:T(8,128)(2,1)S(1)} %add_convert_fusion.6), channel_id=1, source_target_pairs={{0,1},{1,0},{2,3},{3,2},{4,5},{5,4},{6,7},{7,6},{8,9},{9,8},{10,11... | collective-permute-start | bytes 2359304 | tf_op jit(solution)/shard_map/ppermute | solution.py:207
  169.7 137.1 %collective-permute-start.13 = (bf16[4,96,1664]{2,1,0:T(8,128)(2,1)S(1)}, bf16[4,96,1664]{2,1,0:T(8,128)(2,1)S(1)}, u32[]{:S(2)}, u32[]{:S(2)}) collective-permute-start(bf16[4,96,1664]{2,1,0:T(8,128)(2,1)S(1)} %dynamic-slice_bitcast_fusion), channel_id=1, source_target_pairs={{0,2},{2,0},{4,6},{6,4},{8,10},{10,8},{12,14},{14,12},{1,3},{3,1},... | collective-permute-start | bytes 3833864 | tf_op jit(solution)/shard_map/ppermute | solution.py:269
  172.4 13.7 %collective-permute-start.50 = (bf16[96,1536]{1,0:T(8,128)(2,1)S(1)}, bf16[96,1536]{1,0:T(8,128)(2,1)S(1)}, u32[]{:S(2)}, u32[]{:S(2)}) collective-permute-start(bf16[96,1536]{1,0:T(8,128)(2,1)S(1)} %get-tuple-element.76), channel_id=1, source_target_pairs={{0,12},{2,14},{4,0},{6,2},{8,4},{10,6},{12,8},{14,10},{1,13},{3,15... | collective-permute-start | bytes 884744 | tf_op jit(solution)/shard_map/ppermute | solution.py:284
  174.2 26.6 %collective-permute-start.49 = (bf16[96,1536]{1,0:T(8,128)(2,1)S(1)}, bf16[96,1536]{1,0:T(8,128)(2,1)S(1)}, u32[]{:S(2)}, u32[]{:S(2)}) collective-permute-start(bf16[96,1536]{1,0:T(8,128)(2,1)S(1)} %get-tuple-element.77), channel_id=1, source_target_pairs={{0,8},{2,10},{4,12},{6,14},{8,0},{10,2},{12,4},{14,6},{1,9},{3,11}... | collective-permute-start | bytes 884744 | tf_op jit(solution)/shard_map/ppermute | solution.py:284
  183.4 18.7 %collective-permute-start.48 = (bf16[96,1536]{1,0:T(8,128)(2,1)S(1)}, bf16[96,1536]{1,0:T(8,128)(2,1)S(1)}, u32[]{:S(2)}, u32[]{:S(2)}) collective-permute-start(bf16[96,1536]{1,0:T(8,128)(2,1)S(1)} %get-tuple-element.75), channel_id=1, source_target_pairs={{0,4},{2,6},{4,8},{6,10},{8,12},{10,14},{12,0},{14,2},{1,5},{3,7},... | collective-permute-start | bytes 884744 | tf_op jit(solution)/shard_map/ppermute | solution.py:284
  186.1 36.0 %collective-permute-start.37 = (bf16[4,96,768]{2,1,0:T(8,128)(2,1)S(1)}, bf16[4,96,768]{2,1,0:T(8,128)(2,1)S(1)}, u32[]{:S(2)}, u32[]{:S(2)}) collective-permute-start(bf16[4,96,768]{2,1,0:T(8,128)(2,1)S(1)} %dynamic-slice_bitcast_fusion.4), channel_id=1, source_target_pairs={{0,2},{2,0},{4,6},{6,4},{8,10},{10,8},{12,14},{14,12},{1,3},{3,1},... | collective-permute-start | bytes 1769480 | tf_op jit(solution)/shard_map/ppermute | solution.py:269
  200.7 24.4 %collective-permute-start.31 = (bf16[4,96,768]{2,1,0:T(8,128)(2,1)S(1)}, bf16[4,96,768]{2,1,0:T(8,128)(2,1)S(1)}, u32[]{:S(2)}, u32[]{:S(2)}) collective-permute-start(bf16[4,96,768]{2,1,0:T(8,128)(2,1)S(1)} %dynamic-slice_bitcast_fusion.5), channel_id=1, source_target_pairs={{0,2},{2,0},{4,6},{6,4},{8,10},{10,8},{12,14},{14,12},{1,3},{3,1},... | collective-permute-start | bytes 1769480 | tf_op jit(solution)/shard_map/ppermute | solution.py:269
  202.3 24.0 %collective-permute-start.51 = (bf16[96,1536]{1,0:T(8,128)(2,1)S(1)}, bf16[96,1536]{1,0:T(8,128)(2,1)S(1)}, u32[]{:S(2)}, u32[]{:S(2)}) collective-permute-start(bf16[96,1536]{1,0:T(8,128)(2,1)S(1)} %fusion.101), channel_id=1, source_target_pairs={{0,16},{16,0},{1,17},{17,1},{2,18},{18,2},{3,19},{19,3},{4,20},{20... | collective-permute-start | bytes 884744 | tf_op jit(solution)/shard_map/ppermute | solution.py:207
  216.5 95.1 %collective-permute-start.6 = (bf16[512,768]{1,0:T(8,128)(2,1)S(1)}, bf16[512,768]{1,0:T(8,128)(2,1)S(1)}, u32[]{:S(2)}, u32[]{:S(2)}) collective-permute-start(bf16[512,768]{1,0:T(8,128)(2,1)S(1)} %add_convert_fusion.5), channel_id=1, source_target_pairs={{0,1},{1,0},{2,3},{3,2},{4,5},{5,4},{6,7},{7,6},{8,9},{9,8},{10,11... | collective-permute-start | bytes 2359304 | tf_op jit(solution)/shard_map/ppermute | solution.py:207
  222.8 7.6 %collective-permute-start.40 = (bf16[96,768]{1,0:T(8,128)(2,1)S(1)}, bf16[96,768]{1,0:T(8,128)(2,1)S(1)}, u32[]{:S(2)}, u32[]{:S(2)}) collective-permute-start(bf16[96,768]{1,0:T(8,128)(2,1)S(1)} %get-tuple-element.95), channel_id=1, source_target_pairs={{0,12},{2,14},{4,0},{6,2},{8,4},{10,6},{12,8},{14,10},{1,13},{3,15... | collective-permute-start | bytes 442376 | tf_op jit(solution)/shard_map/ppermute | solution.py:284
  225.1 14.1 %collective-permute-start.39 = (bf16[96,768]{1,0:T(8,128)(2,1)S(1)}, bf16[96,768]{1,0:T(8,128)(2,1)S(1)}, u32[]{:S(2)}, u32[]{:S(2)}) collective-permute-start(bf16[96,768]{1,0:T(8,128)(2,1)S(1)} %get-tuple-element.96), channel_id=1, source_target_pairs={{0,8},{2,10},{4,12},{6,14},{8,0},{10,2},{12,4},{14,6},{1,9},{3,11}... | collective-permute-start | bytes 442376 | tf_op jit(solution)/shard_map/ppermute | solution.py:284
  226.3 12.9 %collective-permute-start.38 = (bf16[96,768]{1,0:T(8,128)(2,1)S(1)}, bf16[96,768]{1,0:T(8,128)(2,1)S(1)}, u32[]{:S(2)}, u32[]{:S(2)}) collective-permute-start(bf16[96,768]{1,0:T(8,128)(2,1)S(1)} %get-tuple-element.94), channel_id=1, source_target_pairs={{0,4},{2,6},{4,8},{6,10},{8,12},{10,14},{12,0},{14,2},{1,5},{3,7},... | collective-permute-start | bytes 442376 | tf_op jit(solution)/shard_map/ppermute | solution.py:284
  230.4 14.2 %collective-permute-start.34 = (bf16[96,768]{1,0:T(8,128)(2,1)S(1)}, bf16[96,768]{1,0:T(8,128)(2,1)S(1)}, u32[]{:S(2)}, u32[]{:S(2)}) collective-permute-start(bf16[96,768]{1,0:T(8,128)(2,1)S(1)} %get-tuple-element.92), channel_id=1, source_target_pairs={{0,12},{2,14},{4,0},{6,2},{8,4},{10,6},{12,8},{14,10},{1,13},{3,15... | collective-permute-start | bytes 442376 | tf_op jit(solution)/shard_map/ppermute | solution.py:284
  239.2 11.3 %collective-permute-start.33 = (bf16[96,768]{1,0:T(8,128)(2,1)S(1)}, bf16[96,768]{1,0:T(8,128)(2,1)S(1)}, u32[]{:S(2)}, u32[]{:S(2)}) collective-permute-start(bf16[96,768]{1,0:T(8,128)(2,1)S(1)} %get-tuple-element.93), channel_id=1, source_target_pairs={{0,8},{2,10},{4,12},{6,14},{8,0},{10,2},{12,4},{14,6},{1,9},{3,11}... | collective-permute-start | bytes 442376 | tf_op jit(solution)/shard_map/ppermute | solution.py:284
  239.2 12.5 %collective-permute-start.32 = (bf16[96,768]{1,0:T(8,128)(2,1)S(1)}, bf16[96,768]{1,0:T(8,128)(2,1)S(1)}, u32[]{:S(2)}, u32[]{:S(2)}) collective-permute-start(bf16[96,768]{1,0:T(8,128)(2,1)S(1)} %get-tuple-element.91), channel_id=1, source_target_pairs={{0,4},{2,6},{4,8},{6,10},{8,12},{10,14},{12,0},{14,2},{1,5},{3,7},... | collective-permute-start | bytes 442376 | tf_op jit(solution)/shard_map/ppermute | solution.py:284
  244.6 124.2 %collective-permute-start.24 = (bf16[768,768]{1,0:T(8,128)(2,1)}, bf16[768,768]{1,0:T(8,128)(2,1)}, u32[]{:S(2)}, u32[]{:S(2)}) collective-permute-start(bf16[768,768]{1,0:T(8,128)(2,1)} %constant_dynamic-slice_fusion.3), channel_id=1, source_target_pairs={{0,16},{16,0},{1,17},{17,1},{2,18},{18,2},{3,19},{19,3},{4,20},{20... | collective-permute-start | bytes 3538952 | tf_op jit(solution)/shard_map/ppermute | solution.py:269
  250.5 120.1 %collective-permute-start.18 = (bf16[768,768]{1,0:T(8,128)(2,1)}, bf16[768,768]{1,0:T(8,128)(2,1)}, u32[]{:S(2)}, u32[]{:S(2)}) collective-permute-start(bf16[768,768]{1,0:T(8,128)(2,1)} %constant_dynamic-slice_fusion.4), channel_id=1, source_target_pairs={{0,16},{16,0},{1,17},{17,1},{2,18},{18,2},{3,19},{19,3},{4,20},{20... | collective-permute-start | bytes 3538952 | tf_op jit(solution)/shard_map/ppermute | solution.py:269
  251.7 49.1 %collective-permute-start.41 = (bf16[96,768]{1,0:T(8,128)(2,1)S(1)}, bf16[96,768]{1,0:T(8,128)(2,1)S(1)}, u32[]{:S(2)}, u32[]{:S(2)}) collective-permute-start(bf16[96,768]{1,0:T(8,128)(2,1)S(1)} %fusion.154), channel_id=1, source_target_pairs={{0,16},{16,0},{1,17},{17,1},{2,18},{18,2},{3,19},{19,3},{4,20},{20... | collective-permute-start | bytes 442376 | tf_op jit(solution)/shard_map/ppermute | solution.py:207
  307.2 26.6 %collective-permute-start.16 = (bf16[96,1664]{1,0:T(8,128)(2,1)S(1)}, bf16[96,1664]{1,0:T(8,128)(2,1)S(1)}, u32[]{:S(2)}, u32[]{:S(2)}) collective-permute-start(bf16[96,1664]{1,0:T(8,128)(2,1)S(1)} %get-tuple-element.70), channel_id=1, source_target_pairs={{0,12},{2,14},{4,0},{6,2},{8,4},{10,6},{12,8},{14,10},{1,13},{3,15... | collective-permute-start | bytes 958472 | tf_op jit(solution)/shard_map/ppermute | solution.py:284
  307.3 29.7 %collective-permute-start.15 = (bf16[96,1664]{1,0:T(8,128)(2,1)S(1)}, bf16[96,1664]{1,0:T(8,128)(2,1)S(1)}, u32[]{:S(2)}, u32[]{:S(2)}) collective-permute-start(bf16[96,1664]{1,0:T(8,128)(2,1)S(1)} %get-tuple-element.71), channel_id=1, source_target_pairs={{0,8},{2,10},{4,12},{6,14},{8,0},{10,2},{12,4},{14,6},{1,9},{3,11}... | collective-permute-start | bytes 958472 | tf_op jit(solution)/shard_map/ppermute | solution.py:284
  311.6 25.4 %collective-permute-start.14 = (bf16[96,1664]{1,0:T(8,128)(2,1)S(1)}, bf16[96,1664]{1,0:T(8,128)(2,1)S(1)}, u32[]{:S(2)}, u32[]{:S(2)}) collective-permute-start(bf16[96,1664]{1,0:T(8,128)(2,1)S(1)} %get-tuple-element.69), channel_id=1, source_target_pairs={{0,4},{2,6},{4,8},{6,10},{8,12},{10,14},{12,0},{14,2},{1,5},{3,7},... | collective-permute-start | bytes 958472 | tf_op jit(solution)/shard_map/ppermute | solution.py:284
  333.9 29.2 %collective-permute-start.42 = (bf16[4,96,1536]{2,1,0:T(8,128)(2,1)}, bf16[4,96,1536]{2,1,0:T(8,128)(2,1)}, u32[]{:S(2)}, u32[]{:S(2)}) collective-permute-start(bf16[4,96,1536]{2,1,0:T(8,128)(2,1)} %dynamic-slice_bitcast_fusion.2), channel_id=1, source_target_pairs={{0,2},{2,0},{4,6},{6,4},{8,10},{10,8},{12,14},{14,12},{1,3},{3,1},... | collective-permute-start | bytes 3538952 | tf_op jit(solution)/shard_map/ppermute | solution.py:269
  337.0 51.0 %collective-permute-start.7 = (bf16[512,768]{1,0:T(8,128)(2,1)S(1)}, bf16[512,768]{1,0:T(8,128)(2,1)}, u32[]{:S(2)}, u32[]{:S(2)}) collective-permute-start(bf16[512,768]{1,0:T(8,128)(2,1)S(1)} %add_convert_fusion.4), channel_id=1, source_target_pairs={{0,1},{1,0},{2,3},{3,2},{4,5},{5,4},{6,7},{7,6},{8,9},{9,8},{10,11... | collective-permute-start | bytes 2359304 | tf_op jit(solution)/shard_map/ppermute | solution.py:207
  337.2 10.1 %collective-permute-start.17 = (bf16[96,1664]{1,0:T(8,128)(2,1)S(1)}, bf16[96,1664]{1,0:T(8,128)(2,1)}, u32[]{:S(2)}, u32[]{:S(2)}) collective-permute-start(bf16[96,1664]{1,0:T(8,128)(2,1)S(1)} %fusion.98), channel_id=1, source_target_pairs={{0,16},{16,0},{1,17},{17,1},{2,18},{18,2},{3,19},{19,3},{4,20},{20... | collective-permute-start | bytes 958472 | tf_op jit(solution)/shard_map/ppermute | solution.py:207
  347.3 161.6 %collective-permute-start.8 = (bf16[4,96,1536]{2,1,0:T(8,128)(2,1)}, bf16[4,96,1536]{2,1,0:T(8,128)(2,1)}, u32[]{:S(2)}, u32[]{:S(2)}) collective-permute-start(bf16[4,96,1536]{2,1,0:T(8,128)(2,1)} %dynamic-slice_bitcast_fusion.3), channel_id=1, source_target_pairs={{0,2},{2,0},{4,6},{6,4},{8,10},{10,8},{12,14},{14,12},{1,3},{3,1},... | collective-permute-start | bytes 3538952 | tf_op jit(solution)/shard_map/ppermute | solution.py:269
  364.9 10.3 %collective-permute-start.45 = (bf16[96,1536]{1,0:T(8,128)(2,1)S(1)}, bf16[96,1536]{1,0:T(8,128)(2,1)S(1)}, u32[]{:S(2)}, u32[]{:S(2)}) collective-permute-start(bf16[96,1536]{1,0:T(8,128)(2,1)S(1)} %get-tuple-element.73), channel_id=1, source_target_pairs={{0,12},{2,14},{4,0},{6,2},{8,4},{10,6},{12,8},{14,10},{1,13},{3,15... | collective-permute-start | bytes 884744 | tf_op jit(solution)/shard_map/ppermute | solution.py:284
  368.8 16.6 %collective-permute-start.44 = (bf16[96,1536]{1,0:T(8,128)(2,1)S(1)}, bf16[96,1536]{1,0:T(8,128)(2,1)S(1)}, u32[]{:S(2)}, u32[]{:S(2)}) collective-permute-start(bf16[96,1536]{1,0:T(8,128)(2,1)S(1)} %get-tuple-element.74), channel_id=1, source_target_pairs={{0,8},{2,10},{4,12},{6,14},{8,0},{10,2},{12,4},{14,6},{1,9},{3,11}... | collective-permute-start | bytes 884744 | tf_op jit(solution)/shard_map/ppermute | solution.py:284
  370.5 14.9 %collective-permute-start.43 = (bf16[96,1536]{1,0:T(8,128)(2,1)S(1)}, bf16[96,1536]{1,0:T(8,128)(2,1)S(1)}, u32[]{:S(2)}, u32[]{:S(2)}) collective-permute-start(bf16[96,1536]{1,0:T(8,128)(2,1)S(1)} %get-tuple-element.72), channel_id=1, source_target_pairs={{0,4},{2,6},{4,8},{6,10},{8,12},{10,14},{12,0},{14,2},{1,5},{3,7},... | collective-permute-start | bytes 884744 | tf_op jit(solution)/shard_map/ppermute | solution.py:284
  375.2 105.9 %collective-permute-start.25 = (bf16[4,96,768]{2,1,0:T(8,128)(2,1)}, bf16[4,96,768]{2,1,0:T(8,128)(2,1)}, u32[]{:S(2)}, u32[]{:S(2)}) collective-permute-start(bf16[4,96,768]{2,1,0:T(8,128)(2,1)} %dynamic-slice_bitcast_fusion.6), channel_id=1, source_target_pairs={{0,2},{2,0},{4,6},{6,4},{8,10},{10,8},{12,14},{14,12},{1,3},{3,1},... | collective-permute-start | bytes 1769480 | tf_op jit(solution)/shard_map/ppermute | solution.py:269
  385.4 97.3 %collective-permute-start.19 = (bf16[4,96,768]{2,1,0:T(8,128)(2,1)}, bf16[4,96,768]{2,1,0:T(8,128)(2,1)}, u32[]{:S(2)}, u32[]{:S(2)}) collective-permute-start(bf16[4,96,768]{2,1,0:T(8,128)(2,1)} %dynamic-slice_bitcast_fusion.7), channel_id=1, source_target_pairs={{0,2},{2,0},{4,6},{6,4},{8,10},{10,8},{12,14},{14,12},{1,3},{3,1},... | collective-permute-start | bytes 1769480 | tf_op jit(solution)/shard_map/ppermute | solution.py:269
  386.3 99.6 %collective-permute-start.46 = (bf16[96,1536]{1,0:T(8,128)(2,1)}, bf16[96,1536]{1,0:T(8,128)(2,1)}, u32[]{:S(2)}, u32[]{:S(2)}) collective-permute-start(bf16[96,1536]{1,0:T(8,128)(2,1)} %fusion.104), channel_id=1, source_target_pairs={{0,16},{16,0},{1,17},{17,1},{2,18},{18,2},{3,19},{19,3},{4,20},{20... | collective-permute-start | bytes 884744 | tf_op jit(solution)/shard_map/ppermute | solution.py:207
  482.5 8.1 %collective-permute-start.28 = (bf16[96,768]{1,0:T(8,128)(2,1)S(1)}, bf16[96,768]{1,0:T(8,128)(2,1)S(1)}, u32[]{:S(2)}, u32[]{:S(2)}) collective-permute-start(bf16[96,768]{1,0:T(8,128)(2,1)S(1)} %get-tuple-element.89), channel_id=1, source_target_pairs={{0,12},{2,14},{4,0},{6,2},{8,4},{10,6},{12,8},{14,10},{1,13},{3,15... | collective-permute-start | bytes 442376 | tf_op jit(solution)/shard_map/ppermute | solution.py:284
  482.6 18.8 %collective-permute-start.27 = (bf16[96,768]{1,0:T(8,128)(2,1)S(1)}, bf16[96,768]{1,0:T(8,128)(2,1)S(1)}, u32[]{:S(2)}, u32[]{:S(2)}) collective-permute-start(bf16[96,768]{1,0:T(8,128)(2,1)S(1)} %get-tuple-element.90), channel_id=1, source_target_pairs={{0,8},{2,10},{4,12},{6,14},{8,0},{10,2},{12,4},{14,6},{1,9},{3,11}... | collective-permute-start | bytes 442376 | tf_op jit(solution)/shard_map/ppermute | solution.py:284
  482.7 18.7 %collective-permute-start.26 = (bf16[96,768]{1,0:T(8,128)(2,1)S(1)}, bf16[96,768]{1,0:T(8,128)(2,1)S(1)}, u32[]{:S(2)}, u32[]{:S(2)}) collective-permute-start(bf16[96,768]{1,0:T(8,128)(2,1)S(1)} %get-tuple-element.88), channel_id=1, source_target_pairs={{0,4},{2,6},{4,8},{6,10},{8,12},{10,14},{12,0},{14,2},{1,5},{3,7},... | collective-permute-start | bytes 442376 | tf_op jit(solution)/shard_map/ppermute | solution.py:284
  485.9 15.6 %collective-permute-start.22 = (bf16[96,768]{1,0:T(8,128)(2,1)S(1)}, bf16[96,768]{1,0:T(8,128)(2,1)S(1)}, u32[]{:S(2)}, u32[]{:S(2)}) collective-permute-start(bf16[96,768]{1,0:T(8,128)(2,1)S(1)} %get-tuple-element.86), channel_id=1, source_target_pairs={{0,12},{2,14},{4,0},{6,2},{8,4},{10,6},{12,8},{14,10},{1,13},{3,15... | collective-permute-start | bytes 442376 | tf_op jit(solution)/shard_map/ppermute | solution.py:284
  490.6 18.0 %collective-permute-start.21 = (bf16[96,768]{1,0:T(8,128)(2,1)S(1)}, bf16[96,768]{1,0:T(8,128)(2,1)S(1)}, u32[]{:S(2)}, u32[]{:S(2)}) collective-permute-start(bf16[96,768]{1,0:T(8,128)(2,1)S(1)} %get-tuple-element.87), channel_id=1, source_target_pairs={{0,8},{2,10},{4,12},{6,14},{8,0},{10,2},{12,4},{14,6},{1,9},{3,11}... | collective-permute-start | bytes 442376 | tf_op jit(solution)/shard_map/ppermute | solution.py:284
  501.4 7.2 %collective-permute-start.20 = (bf16[96,768]{1,0:T(8,128)(2,1)S(1)}, bf16[96,768]{1,0:T(8,128)(2,1)S(1)}, u32[]{:S(2)}, u32[]{:S(2)}) collective-permute-start(bf16[96,768]{1,0:T(8,128)(2,1)S(1)} %get-tuple-element.85), channel_id=1, source_target_pairs={{0,4},{2,6},{4,8},{6,10},{8,12},{10,14},{12,0},{14,2},{1,5},{3,7},... | collective-permute-start | bytes 442376 | tf_op jit(solution)/shard_map/ppermute | solution.py:284
  501.5 14.7 %collective-permute-start.29 = (bf16[96,768]{1,0:T(8,128)(2,1)S(1)}, bf16[96,768]{1,0:T(8,128)(2,1)S(1)}, u32[]{:S(2)}, u32[]{:S(2)}) collective-permute-start(bf16[96,768]{1,0:T(8,128)(2,1)S(1)} %fusion.160), channel_id=1, source_target_pairs={{0,16},{16,0},{1,17},{17,1},{2,18},{18,2},{3,19},{19,3},{4,20},{20... | collective-permute-start | bytes 442376 | tf_op jit(solution)/shard_map/ppermute | solution.py:207
  508.7 7.6 %collective-permute-start.23 = (bf16[96,768]{1,0:T(8,128)(2,1)S(1)}, bf16[96,768]{1,0:T(8,128)(2,1)S(1)}, u32[]{:S(2)}, u32[]{:S(2)}) collective-permute-start(bf16[96,768]{1,0:T(8,128)(2,1)S(1)} %fusion.163), channel_id=1, source_target_pairs={{0,16},{16,0},{1,17},{17,1},{2,18},{18,2},{3,19},{19,3},{4,20},{20... | collective-permute-start | bytes 442376 | tf_op jit(solution)/shard_map/ppermute | solution.py:207
  510.6 6.8 %collective-permute-start.11 = (bf16[96,1536]{1,0:T(8,128)(2,1)S(1)}, bf16[96,1536]{1,0:T(8,128)(2,1)S(1)}, u32[]{:S(2)}, u32[]{:S(2)}) collective-permute-start(bf16[96,1536]{1,0:T(8,128)(2,1)S(1)} %get-tuple-element.79), channel_id=1, source_target_pairs={{0,12},{2,14},{4,0},{6,2},{8,4},{10,6},{12,8},{14,10},{1,13},{3,15... | collective-permute-start | bytes 884744 | tf_op jit(solution)/shard_map/ppermute | solution.py:284
  512.0 16.3 %collective-permute-start.10 = (bf16[96,1536]{1,0:T(8,128)(2,1)S(1)}, bf16[96,1536]{1,0:T(8,128)(2,1)S(1)}, u32[]{:S(2)}, u32[]{:S(2)}) collective-permute-start(bf16[96,1536]{1,0:T(8,128)(2,1)S(1)} %get-tuple-element.80), channel_id=1, source_target_pairs={{0,8},{2,10},{4,12},{6,14},{8,0},{10,2},{12,4},{14,6},{1,9},{3,11}... | collective-permute-start | bytes 884744 | tf_op jit(solution)/shard_map/ppermute | solution.py:284
  514.2 14.1 %collective-permute-start.9 = (bf16[96,1536]{1,0:T(8,128)(2,1)S(1)}, bf16[96,1536]{1,0:T(8,128)(2,1)S(1)}, u32[]{:S(2)}, u32[]{:S(2)}) collective-permute-start(bf16[96,1536]{1,0:T(8,128)(2,1)S(1)} %get-tuple-element.78), channel_id=1, source_target_pairs={{0,4},{2,6},{4,8},{6,10},{8,12},{10,14},{12,0},{14,2},{1,5},{3,7},... | collective-permute-start | bytes 884744 | tf_op jit(solution)/shard_map/ppermute | solution.py:284
  528.5 6.8 %collective-permute-start.12 = (bf16[96,1536]{1,0:T(8,128)(2,1)S(1)}, bf16[96,1536]{1,0:T(8,128)(2,1)S(1)}, u32[]{:S(2)}, u32[]{:S(2)}) collective-permute-start(bf16[96,1536]{1,0:T(8,128)(2,1)S(1)} %fusion.107), channel_id=1, source_target_pairs={{0,16},{16,0},{1,17},{17,1},{2,18},{18,2},{3,19},{19,3},{4,20},{20... | collective-permute-start | bytes 884744 | tf_op jit(solution)/shard_map/ppermute | solution.py:207
  (95 other events, 742.6 us)
